TPU v7x, 32 devices: a whole 2x2x4 slice. The times are simulated.
32 devices in a mesh: space: 16 (over z, y, x), sub: 2 (over core).
Axes of the slice: x: 2, y: 2, z: 4, core: 2. Of those that a mesh axis runs over, the one named last changes fastest.
Arguments:
- mode_rows: float32 [256, 262144], P(None, ('space', 'sub')), as said below
- snapshots: float32 [3, 64, 262144], P(None, None, ('space', 'sub')), as said below
- probe_fields: float32 [128, 262144], P(None, ('space', 'sub')), as said below
- core_factor: float32 [256, 256], replicated, as said below
Outputs:
- new_modes: float32 [256, 262144], P(None, ('space', 'sub'))
- new_core: float32 [256, 256], replicated
- captured: float32 [3, 256, 320], replicated
Inputs may be any that keep to these rules, and one draw needn't show every extreme that they name: `mode_rows`: rows of full rank, entries of order one. `snapshots`: fields of order one. `probe_fields`: fields of order one. `core_factor`: lower triangular with a positive diagonal.
All inputs are finite; a program needn't handle non-finite values.
Results may differ from a plain program's by a relative error of at most 0.0003.
Values sent between devices are 32-bit elements; how exact they have to be, the bound alone decides.
No kernel may reach another device: no remote copies, remote signals or barrier semaphores. Data moves between devices by JAX's collectives and lax.ppermute only.
A program may use at most 128 MiB of HBM per device.

v0:
```python
import jax
import jax.numpy as jnp
from jax import lax
from jax.sharding import PartitionSpec as P

TURNS = 2


PRECISE = lax.Precision.HIGHEST


def row_inner(left, right):
    return lax.dot_general(left, right, (((1,), (1,)), ((), ())), precision=PRECISE)


def matmul_high(left, right):
    return jnp.dot(left, right, precision=PRECISE)


def block_cholesky(matrix):
    order = matrix.shape[0]
    width = 64
    lowered = jnp.zeros((order, order), jnp.float32)
    for start in range(0, order, width):
        finish = start + width
        done_rows = lowered[start:finish, :start]
        diag_block = matrix[start:finish, start:finish] - matmul_high(done_rows, done_rows.T)
        diag_factor = jnp.linalg.cholesky(diag_block)
        lowered = lowered.at[start:finish, start:finish].set(diag_factor)
        if finish < order:
            below = matrix[finish:, start:finish] - matmul_high(
                lowered[finish:, :start], done_rows.T
            )
            panel = jax.scipy.linalg.solve_triangular(diag_factor, below.T, lower=True).T
            lowered = lowered.at[finish:, start:finish].set(panel)
    return lowered


def update_core(core_now, projected, factor, turn_count):
    rank_count = core_now.shape[0]
    batch_count = factor.shape[0]
    upper = jnp.concatenate([core_now, projected], axis=1)
    bottom = jnp.concatenate([jnp.zeros((batch_count, rank_count), jnp.float32), factor.T], axis=1)
    stacked = jnp.concatenate([upper, bottom], axis=0)
    squared = matmul_high(stacked, stacked.T)
    rotation = jnp.eye(rank_count + batch_count, rank_count, dtype=jnp.float32)
    for sweep_index in range(turn_count):
        rotation = matmul_high(squared, rotation)
        lowered = block_cholesky(matmul_high(rotation.T, rotation))
        rotation = jax.scipy.linalg.solve_triangular(lowered, rotation.T, lower=True).T
    fresh_core = block_cholesky(matmul_high(rotation.T, matmul_high(squared, rotation)))
    return (rotation, fresh_core)


def orthonormalize(residual, volume):
    gram_local = row_inner(residual, residual)
    factor = block_cholesky(lax.psum(gram_local, ("space", "sub")) * volume)
    orthogonal = jax.scipy.linalg.solve_triangular(factor, residual, lower=True)
    return (factor, orthogonal)


def body(mode_rows, snapshots, probe_fields, core_factor):
    local_rows = mode_rows.shape[1]
    batch_count = snapshots.shape[0]
    batch_width = snapshots.shape[1]
    volume = 1.0 / (local_rows * lax.axis_size("space") * lax.axis_size("sub"))
    window = jnp.concatenate(
        [snapshots.reshape(batch_count * batch_width, local_rows), probe_fields], axis=0
    )
    basis_now = mode_rows
    core_now = core_factor
    captured = []
    for batch_index in range(batch_count):
        incoming = snapshots[batch_index]
        projected = lax.psum(row_inner(basis_now, incoming), ("space", "sub")) * volume
        residual = incoming - matmul_high(projected.T, basis_now)
        factor, orthogonal = orthonormalize(residual, volume)
        rotation, core_now = update_core(core_now, projected, factor, TURNS)
        basis_now = matmul_high(rotation.T, jnp.concatenate([basis_now, orthogonal], axis=0))
        captured.append(lax.psum(row_inner(basis_now, window), ("space", "sub")) * volume)
    return (basis_now, core_now, jnp.stack(captured))


def solution(mesh):
    return jax.shard_map(
        body,
        mesh=mesh,
        in_specs=(
            P(None, ("space", "sub")),
            P(None, None, ("space", "sub")),
            P(None, ("space", "sub")),
            P(),
        ),
        out_specs=(P(None, ("space", "sub")), P(), P()),
        check_vma=False,
    )
```

profile of v0, /device:TPU:0, one launch (start us, length us, event | category | flops | bytes accessed | tf_op | source)
XLA Modules:
  0.0 1490.3 jit_solution(688656669866002089)
XLA Ops:
  7.2 10.0 fusion.19
  17.3 125.2 %all-reduce.18.cloned.1.call-done = f32[256,64]{1,0:T(8,128)} async-done(((f32[256,64]{1,0:T(8,128)}), f32[256,64]{1,0:T(8,128)}) %all-reduce.18.cloned.1.call-update) | async-done | bytes 65552 | tf_op jit(solution)/shard_map/psum | solution.py:75
  142.5 9.2 convolution_subtract_fusion.2
  153.4 39.6 %psum.64 = f32[64,64]{0,1:T(8,128)S(1)} all-reduce(f32[64,64]{0,1:T(8,128)S(1)} %fusion.442), channel_id=1, replica_groups=mesh['space'=16,'sub'=2] {'space','sub'}, use_global_device_ids=true, to_apply=%region_1.0 | all-reduce | flops 4096 | bytes 32768 | tf_op jit(solution)/shard_map/psum | solution.py:57
  193.1 5.8 cholesky.599
  203.4 5.8 cholesky.610
  237.9 5.8 cholesky.632
  254.1 5.8 cholesky.643
  266.4 19.7 %custom-call.51 = f32[2,128,128]{1,2,0:T(8,128)S(1)} custom-call(f32[2,128,128]{2,1,0:T(8,128)S(1)} %get-tuple-element.863), custom_call_target="InvertDiagBlocksLowerTriangular" | custom-call | tf_op jit(solution)/shard_map/jit(_solve_triangular)/triangular_solve | solution.py:50
  288.6 5.8 cholesky.654
  302.1 5.8 cholesky.665
  342.1 5.8 cholesky.687
  356.0 19.9 %custom-call.55 = f32[2,128,128]{1,2,0:T(8,128)S(1)} custom-call(f32[2,128,128]{2,1,0:T(8,128)S(1)} %get-tuple-element.864), custom_call_target="InvertDiagBlocksLowerTriangular" | custom-call | tf_op jit(solution)/shard_map/jit(_solve_triangular)/triangular_solve | solution.py:50
  378.5 5.8 cholesky.698
  417.9 5.8 cholesky.720
  432.1 5.8 cholesky.731
  438.7 16.4 %fusion = f32[256,8192]{1,0:T(8,128)S(1)} fusion(f32[64,8192]{1,0:T(8,128)} %fusion.189, f32[256,8192]{1,0:T(8,128)} %param.153, f32[128,320]{0,1:T(8,128)S(1)} %fusion.125, f32[128,320]{0,1:T(8,128)S(1)} %fusion.98), kind=kOutput, calls=%fused_computation.12 | convolution fusion | flops 8055767040 | bytes 19202048 | tf_op jit(solution)/shard_map/dot_general | solution.py:17
  458.4 8.9 fusion.17
  467.4 13.3 fusion.14
  482.4 107.4 %all-reduce.20.cloned.1.call-done = f32[256,64]{1,0:T(8,128)} async-done(((f32[256,64]{1,0:T(8,128)}), f32[256,64]{1,0:T(8,128)}) %all-reduce.20.cloned.1.call-update) | async-done | bytes 65552 | tf_op jit(solution)/shard_map/psum | solution.py:75
  589.8 9.2 convolution_subtract_fusion.1
  600.8 39.6 %psum.66 = f32[64,64]{0,1:T(8,128)S(1)} all-reduce(f32[64,64]{0,1:T(8,128)S(1)} %fusion.445), channel_id=1, replica_groups=mesh['space'=16,'sub'=2] {'space','sub'}, use_global_device_ids=true, to_apply=%region_5.12 | all-reduce | flops 4096 | bytes 32768 | tf_op jit(solution)/shard_map/psum | solution.py:57
  640.5 5.8 cholesky.742
  650.8 5.8 cholesky.753
  664.3 5.8 cholesky.764
  701.7 5.8 cholesky.786
  714.0 19.7 %custom-call.63 = f32[2,128,128]{1,2,0:T(8,128)S(1)} custom-call(f32[2,128,128]{2,1,0:T(8,128)S(1)} %get-tuple-element.865), custom_call_target="InvertDiagBlocksLowerTriangular" | custom-call | tf_op jit(solution)/shard_map/jit(_solve_triangular)/triangular_solve | solution.py:50
  736.2 5.8 cholesky.797
  749.7 5.8 cholesky.808
  789.9 5.8 cholesky.830
  803.8 19.9 %custom-call.67 = f32[2,128,128]{1,2,0:T(8,128)S(1)} custom-call(f32[2,128,128]{2,1,0:T(8,128)S(1)} %get-tuple-element.866), custom_call_target="InvertDiagBlocksLowerTriangular" | custom-call | tf_op jit(solution)/shard_map/jit(_solve_triangular)/triangular_solve | solution.py:50
  826.2 5.8 cholesky.841
  864.0 17.7 %fusion.4 = f32[256,8192]{1,0:T(8,128)S(1)} fusion(f32[64,8192]{1,0:T(8,128)S(1)} %fusion.165, f32[256,8192]{1,0:T(8,128)} %copy-done.1, f32[128,320]{0,1:T(8,128)S(1)} %fusion.115, f32[128,320]{0,1:T(8,128)S(1)} %fusion.94), kind=kOutput, calls=%fused_computation.16 | convolution fusion | flops 8055767040 | bytes 19202048 | tf_op jit(solution)/shard_map/dot_general | solution.py:17
  884.9 8.9 fusion.15
  893.8 13.1 fusion.13
  907.3 5.8 cholesky.863
  921.6 5.8 cholesky.874
  929.7 100.0 %all-reduce.22.cloned.1.call-done = f32[256,64]{1,0:T(8,128)} async-done(((f32[256,64]{1,0:T(8,128)}), f32[256,64]{1,0:T(8,128)}) %all-reduce.22.cloned.1.call-update) | async-done | bytes 65552 | tf_op jit(solution)/shard_map/psum | solution.py:75
  1029.7 9.2 convolution_subtract_fusion
  1040.7 39.6 %psum.68 = f32[64,64]{0,1:T(8,128)S(1)} all-reduce(f32[64,64]{0,1:T(8,128)S(1)} %fusion.448), channel_id=1, replica_groups=mesh['space'=16,'sub'=2] {'space','sub'}, use_global_device_ids=true, to_apply=%region_7.14 | all-reduce | flops 4096 | bytes 32768 | tf_op jit(solution)/shard_map/psum | solution.py:57
  1090.7 5.8 cholesky.896
  1153.6 19.7 %custom-call.75 = f32[2,128,128]{1,2,0:T(8,128)S(1)} custom-call(f32[2,128,128]{2,1,0:T(8,128)S(1)} %get-tuple-element.867), custom_call_target="InvertDiagBlocksLowerTriangular" | custom-call | tf_op jit(solution)/shard_map/jit(_solve_triangular)/triangular_solve | solution.py:50
  1175.8 5.8 cholesky.940
  1243.4 19.9 %custom-call.79 = f32[2,128,128]{1,2,0:T(8,128)S(1)} custom-call(f32[2,128,128]{2,1,0:T(8,128)S(1)} %get-tuple-element.868), custom_call_target="InvertDiagBlocksLowerTriangular" | custom-call | tf_op jit(solution)/shard_map/jit(_solve_triangular)/triangular_solve | solution.py:50
  1265.8 5.8 cholesky.984
  1303.6 18.6 %fusion.8 = f32[256,8192]{1,0:T(8,128)} fusion(f32[64,8192]{1,0:T(8,128)S(1)} %fusion.148, f32[256,8192]{1,0:T(8,128)} %copy-done, f32[128,320]{0,1:T(8,128)S(1)} %fusion.105, f32[128,320]{0,1:T(8,128)S(1)} %fusion.90), kind=kOutput, calls=%fused_computation.20 | convolution fusion | flops 8055767040 | bytes 19202048 | tf_op jit(solution)/shard_map/dot_general | solution.py:17
  1336.5 13.4 fusion.12
  1358.1 122.0 %all-reduce.24.cloned.1.call-done = (f32[256,320]{0,1:T(8,128)}, f32[256,320]{0,1:T(8,128)}, f32[256,320]{0,1:T(8,128)}) async-done(((f32[256,320]{0,1:T(8,128)}, f32[256,320]{0,1:T(8,128)}, f32[256,320]{0,1:T(8,128)}), (f32[256,320]{0,1:T(8,128)}, f32[256,320]{0,1:T(8,128)}, f32[256,320]{0,1:T(8,128)})) %all-reduce.24.cloned.1.call-update) | async-done | bytes 983056 | tf_op jit(solution)/shard_map/psum | solution.py:80
  (535 shorter events, 522.7 us)
Async XLA Ops:
  7.2 135.3 %all-reduce.18.cloned.1.call-start = ((), (), s32[]{:S(2)}) async-start(), calls=%async_computation | async-start | bytes 262144 | tf_op jit(solution)/shard_map/psum | solution.py:75
  17.2 572.6 %all-reduce.20.cloned.1.call-start = ((), (), s32[]{:S(2)}) async-start(), calls=%async_computation.1 | async-start | bytes 262144 | tf_op jit(solution)/shard_map/psum | solution.py:75
  17.2 183.8 %copy-start.9 = (f32[256,256]{1,0:T(8,128)S(1)}, f32[256,256]{1,0:T(8,128)}, u32[]{:S(2)}) copy-start(f32[256,256]{1,0:T(8,128)} %param.156) | copy-start | bytes 786436
  142.5 58.5 %copy-start.6 = (f32[256,64]{1,0:T(8,128)S(1)}, f32[256,64]{1,0:T(8,128)}, u32[]{:S(2)}) copy-start(f32[256,64]{1,0:T(8,128)} %all-reduce.18.cloned.1.call-done) | copy-start | bytes 196612
  203.3 34.3 %copy-start.2 = (f32[256,256]{0,1:T(8,128)}, f32[256,256]{0,1:T(8,128)S(1)}, u32[]{:S(2)}) copy-start(f32[256,256]{0,1:T(8,128)S(1)} %fusion.443) | copy-start | bytes 786436
  455.0 3.4 copy-start.1
  467.4 562.4 %all-reduce.22.cloned.1.call-start = ((), (), s32[]{:S(2)}) async-start(), calls=%async_computation.2 | async-start | bytes 262144 | tf_op jit(solution)/shard_map/psum | solution.py:75
  589.8 58.5 %copy-start.7 = (f32[256,64]{1,0:T(8,128)S(1)}, f32[256,64]{1,0:T(8,128)}, u32[]{:S(2)}) copy-start(f32[256,64]{1,0:T(8,128)} %all-reduce.20.cloned.1.call-done) | copy-start | bytes 196612
  650.6 34.4 %copy-start.3 = (f32[256,256]{0,1:T(8,128)}, f32[256,256]{0,1:T(8,128)S(1)}, u32[]{:S(2)}) copy-start(f32[256,256]{0,1:T(8,128)S(1)} %fusion.446) | copy-start | bytes 786436
  881.7 3.2 copy-start
  907.0 573.2 %all-reduce.24.cloned.1.call-start = ((), (), s32[]{:S(2)}) async-start(), calls=%async_computation.3 | async-start | bytes 1966080 | tf_op jit(solution)/shard_map/psum | solution.py:80
  1029.7 58.5 %copy-start.5 = (f32[256,64]{1,0:T(8,128)S(1)}, f32[256,64]{1,0:T(8,128)}, u32[]{:S(2)}) copy-start(f32[256,64]{1,0:T(8,128)} %all-reduce.22.cloned.1.call-done) | copy-start | bytes 196612
  1090.6 34.2 %copy-start.4 = (f32[256,256]{0,1:T(8,128)}, f32[256,256]{0,1:T(8,128)S(1)}, u32[]{:S(2)}) copy-start(f32[256,256]{0,1:T(8,128)S(1)} %fusion.449) | copy-start | bytes 786436
  1358.1 125.2 %copy-start.8 = (f32[256,256]{1,0:T(8,128)}, f32[256,256]{1,0:T(8,128)S(1)}, u32[]{:S(2)}) copy-start(f32[256,256]{1,0:T(8,128)S(1)} %scatter.314) | copy-start | bytes 786436
Sparse Core Ops, SparseCore 0:
  17.3 125.1 all-reduce.17
  467.5 122.2 all-reduce.19
  907.1 122.5 all-reduce.21
  1350.1 130.0 all-reduce.23
where the time goes:
time: 1500 us; the launch traced here: 1490 us
  other arithmetic  567 us (38%)
  waiting for transfers between devices  455 us (30%)
  matrix products  213 us (14%)
  local copies, waits for them, and re-layouts  119 us (8%)
  blocking collectives  119 us (8%)
  between operations  16.9 us (1%)
    psum x3, waiting for transfers between devices, body(): lax.psum(row_inner(basis_now, incoming), ('space', 'sub')) * volume  333 us
    another operation x117, other arithmetic, block_cholesky(): diag_factor = jnp.linalg.cholesky(diag_block)  255 us
    another operation x54, other arithmetic, block_cholesky(): jax.scipy.linalg.solve_triangular(diag_factor, below.T, lower=True)  161 us
    psum x1, waiting for transfers between devices, body(): lax.psum(row_inner(basis_now, window), ('space', 'sub')) * volume  122 us
    another operation x13, other arithmetic, update_core(): jax.scipy.linalg.solve_triangular(lowered, rotation.T, lower=True)  122 us
    psum x3, blocking collectives, orthonormalize(): factor = block_cholesky(lax.psum(gram_local, ('space', 'sub')) * volume)  119 us
    dot_general x72, matrix products, matmul_high(): return jnp.dot(left, right, precision=PRECISE)  115 us
    dot_general x9, matrix products, row_inner(): lax.dot_general(left, right, (((1,), (1,)), ((), ())), precision=PRECISE)  73 us
  transfers between devices with their start and end apart: 4, of which 4 were waited for; matrix products, arithmetic and copies ran while one was open for 3% of the time, Pallas kernels for 0%

commit v1 on v0

v1 whole, which is shorter than its diff:
```python
import functools

import jax
import jax.numpy as jnp
from jax import lax
from jax.experimental import pallas as pl
from jax.experimental.pallas import tpu as pltpu
from jax.sharding import PartitionSpec as P

TURNS = 2
AXES = ("space", "sub")
FULL = lax.Precision.HIGHEST
LANES = 128
GROUP = 8
PANEL = 64


def nn(left, right):
    return lax.dot_general(
        left, right, (((1,), (0,)), ((), ())), precision=FULL, preferred_element_type=jnp.float32
    )


def nt(left, right):
    return lax.dot_general(
        left, right, (((1,), (1,)), ((), ())), precision=FULL, preferred_element_type=jnp.float32
    )


def tn(left, right):
    return lax.dot_general(
        left, right, (((0,), (0,)), ((), ())), precision=FULL, preferred_element_type=jnp.float32
    )


def wide(column, order):
    return jnp.concatenate([column] * (order // LANES), axis=1)


def inverse_factor(matrix):
    order = matrix.shape[0]
    lane = lax.broadcasted_iota(jnp.int32, (GROUP, order), 1)
    row = lax.broadcasted_iota(jnp.int32, (GROUP, order), 0)
    row_one = lax.broadcasted_iota(jnp.int32, (GROUP, LANES), 0)
    finished = []
    groups = PANEL // GROUP
    for start in range(0, order, PANEL):
        finish = start + PANEL
        held = [matrix[g * GROUP:(g + 1) * GROUP, :] for g in range(groups)]
        panel = []
        for g0 in range(groups):
            first = start + g0 * GROUP
            spread = [
                [
                    jnp.broadcast_to(held[g][:, first + j:first + j + 1], (GROUP, LANES))
                    for g in range(g0, groups)
                ]
                for j in range(GROUP)
            ]
            inside = (lane >= first) & (lane < first + GROUP)
            held[g0] = jnp.where(inside, jnp.where(lane - first == row, 1.0, 0.0), held[g0])
            for g in range(g0 + 1, groups):
                held[g] = jnp.where(inside, 0.0, held[g])
            pivot_column = jnp.ones((GROUP, LANES), jnp.float32)
            factors = []
            for j in range(GROUP):
                pivot = jnp.broadcast_to(spread[j][0][j:j + 1, :], (GROUP, LANES))
                inverse = pltpu.reciprocal(pivot, approx=True)
                inverse = inverse * (2.0 - pivot * inverse)
                pivot_column = jnp.where(row_one == j, pivot, pivot_column)
                factor = [block * inverse for block in spread[j]]
                for later in range(j + 1, GROUP):
                    across = jnp.broadcast_to(spread[later][0][j:j + 1, :], (GROUP, LANES))
                    for t in range(groups - g0):
                        spread[later][t] = spread[later][t] - factor[t] * across
                factor[0] = jnp.where(row_one > j, factor[0], 0.0)
                factors.append(factor)
            for j in range(GROUP):
                pivot_row = jnp.broadcast_to(held[g0][j:j + 1, :], (GROUP, order))
                for t in range(groups - g0):
                    held[g0 + t] = held[g0 + t] - wide(factors[j][t], order) * pivot_row
            panel.append(held[g0] * wide(lax.rsqrt(pivot_column), order))
        finished.extend(panel)
        if finish < order:
            scaled = jnp.concatenate(
                [
                    jnp.where((lane >= start + GROUP * (g + 1)) & (lane < finish), 0.0, panel[g])
                    for g in range(groups)
                ],
                axis=0,
            )
            rest = matrix[PANEL:, :]
            rest_lane = lax.broadcasted_iota(jnp.int32, rest.shape, 1)
            rest = jnp.where((rest_lane >= start) & (rest_lane < finish), 0.0, rest)
            matrix = rest - tn(scaled[:, finish:], scaled)
    lowered = jnp.concatenate(finished, axis=0)
    lane = lax.broadcasted_iota(jnp.int32, lowered.shape, 1)
    row = lax.broadcasted_iota(jnp.int32, lowered.shape, 0)
    return jnp.where(lane <= row, lowered, 0.0)


def lower_factor(matrix):
    lowered = nt(matrix, inverse_factor(matrix))
    lane = lax.broadcasted_iota(jnp.int32, lowered.shape, 1)
    row = lax.broadcasted_iota(jnp.int32, lowered.shape, 0)
    return jnp.where(lane <= row, lowered, 0.0)


def split(values):
    high = values.astype(jnp.bfloat16)
    low = (values - high.astype(jnp.float32)).astype(jnp.bfloat16)
    return high, low


def nt_pass(left, right):
    return lax.dot_general(
        left, right, (((1,), (1,)), ((), ())), preferred_element_type=jnp.float32
    )


def packed_rows(rank, snap_count, batches):
    own = 3 * (rank // 2)
    return own + (rank + snap_count) * (batches - 1) + (rank + snap_count) // 2


def fold(block):
    half = block.shape[0] // 2
    return jnp.concatenate([block[:half, :LANES // 2], block[half:, :LANES // 2]], axis=1)


def unfold(block):
    zeros = jnp.zeros((block.shape[0], LANES // 2), jnp.float32)
    return jnp.concatenate(
        [
            jnp.concatenate([block[:, :LANES // 2], zeros], axis=1),
            jnp.concatenate([block[:, LANES // 2:], zeros], axis=1),
        ],
        axis=0,
    )


def gram_kernel(scale, modes_ref, snaps_ref, probes_ref, packed_ref, modes_out, snaps_out):
    step = pl.program_id(0)

    @pl.when(step == 0)
    def _():
        modes_out[...] = jnp.zeros_like(modes_out)
        snaps_out[...] = jnp.zeros_like(snaps_out)

    count, width, columns = snaps_ref.shape
    probe_count = probes_ref.shape[0]
    spare = LANES - width
    pieces = []
    for batch in range(count):
        pieces.append(snaps_ref[batch])
        taken = min(max(probe_count - batch * spare, 0), spare)
        if taken:
            pieces.append(probes_ref[batch * spare:batch * spare + taken, :])
        if taken < spare:
            pieces.append(jnp.zeros((spare - taken, columns), jnp.float32))
    high, low = split(modes_ref[...])
    field_high, field_low = split(jnp.concatenate(pieces, axis=0))
    all_high = jnp.concatenate([high, field_high], axis=0)
    all_low = jnp.concatenate([low, field_low], axis=0)
    modes_out[...] += nt_pass(high, all_high) + (nt_pass(high, all_low) + nt_pass(low, all_high))
    snap_high, snap_low = split(snaps_ref[...].reshape(count * width, columns))
    snaps_out[...] += nt_pass(snap_high, field_high) + (
        nt_pass(snap_high, field_low) + nt_pass(snap_low, field_high)
    )

    @pl.when(step == pl.num_programs(0) - 1)
    def _():
        rank = modes_ref.shape[0]
        half = rank // 2
        blocks = [
            modes_out[:half, :half],
            modes_out[half:, :half],
            modes_out[half:, half:rank],
        ]
        for batch in range(count):
            tile = slice(rank + batch * LANES, rank + (batch + 1) * LANES)
            block = modes_out[:, tile]
            blocks.append(block if batch + 1 < count else fold(block))
        for batch in range(count):
            block = snaps_out[:, batch * LANES:(batch + 1) * LANES]
            blocks.append(block if batch + 1 < count else fold(block))
        at = 0
        for block in blocks:
            packed_ref[at:at + block.shape[0], :] = block * scale
            at += block.shape[0]


def local_grams(modes, snaps, probes, scale):
    rank, columns = modes.shape
    count, width, _ = snaps.shape
    probe_count = probes.shape[0]
    fields = count * LANES
    tile = 1024
    rows = packed_rows(rank, count * width, count)
    return pl.pallas_call(
        functools.partial(gram_kernel, scale),
        grid=(columns // tile,),
        in_specs=[
            pl.BlockSpec((rank, tile), lambda i: (0, i)),
            pl.BlockSpec((count, width, tile), lambda i: (0, 0, i)),
            pl.BlockSpec((probe_count, tile), lambda i: (0, i)),
        ],
        out_specs=pl.BlockSpec((rows, LANES), lambda i: (0, 0)),
        out_shape=jax.ShapeDtypeStruct((rows, LANES), jnp.float32),
        scratch_shapes=[
            pltpu.VMEM((rank, rank + fields), jnp.float32),
            pltpu.VMEM((count * width, fields), jnp.float32),
        ],
        compiler_params=pltpu.CompilerParams(vmem_limit_bytes=48 << 20),
        name="grams",
    )(modes, snaps, probes)


def sum_over_devices(part, size):
    def swap(value, bit):
        return lax.ppermute(value, AXES, [(i, i ^ bit) for i in range(size)])

    bits = size.bit_length() - 1
    if size != 1 << bits or bits < 2:
        return lax.psum(part, AXES)
    odd = lax.rem(lax.axis_index(AXES), 2) == 1
    half = part.shape[0] // 2
    low, high = part[:half], part[half:]
    part = jnp.where(odd, high, low) + swap(jnp.where(odd, low, high), 1)
    order = list(range(1, bits))
    chunk = -(-half // (3 * GROUP)) * GROUP
    chunks = [part[at:at + chunk] for at in range(0, half, chunk)]
    for turn in range(bits - 1):
        chunks = [
            piece + swap(piece, 1 << order[(turn + number) % len(order)])
            for number, piece in enumerate(chunks)
        ]
    part = jnp.concatenate(chunks, axis=0)
    other = swap(part, 1)
    return jnp.concatenate([jnp.where(odd, other, part), jnp.where(odd, part, other)], axis=0)


def first_lanes(values, width):
    lane = lax.broadcasted_iota(jnp.int32, values.shape, 1)
    return jnp.where(lane < width, values, 0.0)


def product(left, right, across):
    dims = (((1,), (1 if across else 0,)), ((), ()))

    def one(a, b):
        return lax.dot_general(a, b, dims, preferred_element_type=jnp.float32)

    return one(left[0], right[0]) + (one(left[0], right[1]) + one(left[1], right[0]))


def core_kernel(
    packed_ref, core_ref, mix_ref, core_out, captured_ref, energy_ref, norms_ref, inner_ref, snaps_ref, kept_ref
):
    rank = core_ref.shape[0]
    batches = captured_ref.shape[0]
    width = snaps_ref.shape[0] // batches
    probes = captured_ref.shape[2] - batches * width
    half = rank // 2
    norms_ref[:half, :half] = packed_ref[:half, :]
    norms_ref[half:, :half] = packed_ref[half:rank, :]
    norms_ref[:half, half:] = packed_ref[half:rank, :].T
    norms_ref[half:, half:] = packed_ref[rank:rank + half, :]
    at = rank + half
    for target_ref in (inner_ref, snaps_ref):
        count = target_ref.shape[0]
        for batch in range(batches):
            tile = slice(batch * LANES, (batch + 1) * LANES)
            if batch + 1 < batches:
                target_ref[:, tile] = packed_ref[at:at + count, :]
                at += count
            else:
                target_ref[:, tile] = unfold(packed_ref[at:at + count // 2, :])
                at += count // 2
    energy_ref[...] = nt(core_ref[...], core_ref[...])
    lane = lax.broadcasted_iota(jnp.int32, kept_ref.shape, 1)
    row = lax.broadcasted_iota(jnp.int32, kept_ref.shape, 0)
    kept_ref[...] = jnp.where(lane == row, 1.0, 0.0)
    spare = jnp.zeros((LANES - width, LANES), jnp.float32)

    def absorb(batch, carry):
        tile = pl.ds(pl.multiple_of(batch * LANES, LANES), LANES)
        own_rows = pl.ds(pl.multiple_of(batch * width, GROUP), width)
        own = jnp.concatenate([first_lanes(snaps_ref[own_rows, tile], width), spare], axis=0)
        projected = first_lanes(inner_ref[:, tile], width)
        projected_s = split(projected)
        norms = split(norms_ref[...])
        crossed = tn(projected, projected)
        residual = own - crossed - crossed + tn(projected, product(norms, projected_s, False))
        residual_s = split(residual)
        top = energy_ref[...] + product(projected_s, projected_s, True)
        top_s = split(top)
        coupling_s = split(product(projected_s, residual_s, False))
        gram = product(top_s, top_s, True) + product(coupling_s, projected_s, True)
        inverse = split(inverse_factor(gram))
        first_rows = split(product(inverse, top_s, False))
        first_low = split(product(inverse, projected_s, False))
        turned_rows = product(first_rows, top_s, False) + product(first_low, coupling_s, True)
        turned_low = product(first_rows, projected_s, False) + product(first_low, residual_s, False)
        gram = nt(turned_rows, turned_rows) + nt(nn(turned_low, residual), turned_low)
        inverse = inverse_factor(gram)
        rows = nn(inverse, turned_rows)
        low = nn(inverse, turned_low)
        rows_s = split(rows)
        low_s = split(low)
        low_residual = product(low_s, residual_s, False)
        applied_rows = product(rows_s, top_s, False) + product(low_s, coupling_s, True)
        applied_low = product(rows_s, projected_s, False) + low_residual
        energy_ref[...] = product(split(applied_rows), rows_s, True) + product(
            split(applied_low), split(low_residual), True
        )
        old = split(rows - product(low_s, projected_s, True))
        with_window = jnp.concatenate(
            [snaps_ref[own_rows, :], jnp.zeros((LANES - width, snaps_ref.shape[1]), jnp.float32)], axis=0
        )
        inner_ref[...] = product(old, split(inner_ref[...]), False) + product(low_s, split(with_window), False)
        across = product(old, norms, False) + product(low_s, projected_s, True)
        norms_ref[...] = product(split(across), old, True) + product(
            split(first_lanes(inner_ref[:, tile], width)), low_s, True
        )
        kept_ref[...] = product(old, split(kept_ref[...]), False)
        kept_ref[:, pl.ds(pl.multiple_of(rank + batch * LANES, LANES), LANES)] = low
        captured_ref[batch] = jnp.concatenate(
            [inner_ref[:, b * LANES:b * LANES + width] for b in range(batches)]
            + [
                inner_ref[:, b * LANES + width:(b + 1) * LANES]
                for b in range(probes // (LANES - width))
            ],
            axis=1,
        )
        return carry

    lax.fori_loop(0, batches, absorb, 0)
    mix_ref[...] = jnp.concatenate(
        [kept_ref[:, :rank]]
        + [kept_ref[:, rank + b * LANES:rank + b * LANES + width] for b in range(batches)],
        axis=1,
    )
    core_out[...] = lower_factor(energy_ref[...])


def small_algebra(packed, core, batches, width, probes):
    rank = core.shape[0]
    snap_count = batches * width
    columns = batches * LANES
    return pl.pallas_call(
        core_kernel,
        out_shape=[
            jax.ShapeDtypeStruct((rank, rank + snap_count), jnp.float32),
            jax.ShapeDtypeStruct((rank, rank), jnp.float32),
            jax.ShapeDtypeStruct((batches, rank, snap_count + probes), jnp.float32),
        ],
        scratch_shapes=[
            pltpu.VMEM((rank, rank), jnp.float32),
            pltpu.VMEM((rank, rank), jnp.float32),
            pltpu.VMEM((rank, columns), jnp.float32),
            pltpu.VMEM((snap_count, columns), jnp.float32),
            pltpu.VMEM((rank, rank + columns), jnp.float32),
        ],
        compiler_params=pltpu.CompilerParams(vmem_limit_bytes=48 << 20),
        name="core_updates",
    )(packed, core)


def apply_kernel(mix_ref, modes_ref, snaps_ref, out_ref):
    count, width, columns = snaps_ref.shape
    rows = jnp.concatenate([modes_ref[...], snaps_ref[...].reshape(count * width, columns)], axis=0)
    high, low = split(rows)
    mix_high, mix_low = split(mix_ref[...])

    def one(left, right):
        return lax.dot_general(
            left, right, (((1,), (0,)), ((), ())), preferred_element_type=jnp.float32
        )

    out_ref[...] = one(mix_high, high) + (one(mix_high, low) + one(mix_low, high))


def apply_mix(mix, modes, snaps):
    rank, columns = modes.shape
    count, width, _ = snaps.shape
    tile = 1024
    return pl.pallas_call(
        apply_kernel,
        grid=(columns // tile,),
        in_specs=[
            pl.BlockSpec(mix.shape, lambda i: (0, 0)),
            pl.BlockSpec((rank, tile), lambda i: (0, i)),
            pl.BlockSpec((count, width, tile), lambda i: (0, 0, i)),
        ],
        out_specs=pl.BlockSpec((rank, tile), lambda i: (0, i)),
        out_shape=jax.ShapeDtypeStruct((rank, columns), jnp.float32),
        compiler_params=pltpu.CompilerParams(vmem_limit_bytes=48 << 20),
        name="new_basis",
    )(mix, modes, snaps)


def body(modes, snaps, probes, core, *, devices):
    rank, columns = modes.shape
    batches, width, _ = snaps.shape
    scale = 1.0 / (columns * devices)
    packed = sum_over_devices(local_grams(modes, snaps, probes, scale), devices)
    mix, new_core, captured = small_algebra(packed, core, batches, width, probes.shape[0])
    return apply_mix(mix, modes, snaps), new_core, captured


def solution(mesh):
    devices = mesh.shape["space"] * mesh.shape["sub"]
    return jax.shard_map(
        functools.partial(body, devices=devices),
        mesh=mesh,
        in_specs=(P(None, AXES), P(None, None, AXES), P(None, AXES), P()),
        out_specs=(P(None, AXES), P(), P()),
        check_vma=False,
    )
```

time: 1500 us -> 158 us (0.11)
  other arithmetic: 567 us -> 0.48 us
  waiting for transfers between devices: 455 us -> 23 us
  matrix products: 213 us -> 0 us
  blocking collectives: 119 us -> 0 us
  local copies, waits for them, and re-layouts: 119 us -> 3.51 us
  Pallas kernels: 0 us -> 113 us
  between operations: 16.9 us -> 0.79 us
  starting transfers between devices: 0.34 us -> 16.4 us
    another operation x190 -> x0, other arithmetic: 557 us -> none  [the longest x117 255 us: block_cholesky(): diag_factor = jnp.linalg.cholesky(diag_block)]
    psum x4 -> x0, waiting for transfers between devices: 455 us -> none  [the longest x3 333 us: body(): lax.psum(row_inner(basis_now, incoming), ('space', 'sub')) * volume]
    dot_general x81 -> x0, matrix products: 188 us -> none  [the longest x72 115 us: matmul_high(): return jnp.dot(left, right, precision=PRECISE)]
    psum x3 -> x0, blocking collectives: 119 us -> none  [orthonormalize(): factor = block_cholesky(lax.psum(gram_local, ('space', 'sub')) * volume)]
    pallas_call x0 -> x3, Pallas kernels: none -> 113 us  [the longest x1 80.8 us: small_algebra(): pl.pallas_call(core_kernel, out_shape=[jax.ShapeDtypeStruct((rank, rank +...]
    scatter x63 -> x0, local copies, waits for them, and re-layouts: 82.8 us -> none  [the longest x36 47.2 us: block_cholesky(): lowered = lowered.at[start:finish, start:finish].set(diag_factor)]
    another operation x48 -> x0, matrix products: 25.5 us -> none  [the longest x27 13.1 us: block_cholesky(): jax.scipy.linalg.solve_triangular(diag_factor, below.T, lower=True)]
    another operation x43 -> x0, local copies, waits for them, and re-layouts: 23.9 us -> none  [update_core(): jax.scipy.linalg.solve_triangular(lowered, rotation.T, lower=True)]
  transfers between devices with their start and end apart: 4 -> 14, of which waited for: 4 -> 8; matrix products, arithmetic and copies ran while one was open for 3% -> 0% of each run, Pallas kernels for 0% -> 0%
where the time goes in v1:
time: 158 us
  Pallas kernels  113 us (72%)
  waiting for transfers between devices  23 us (15%)
  starting transfers between devices  16.4 us (10%)
  local copies, waits for them, and re-layouts  3.51 us (2%)
    pallas_call x1, Pallas kernels, small_algebra(): pl.pallas_call(core_kernel, out_shape=[jax.ShapeDtypeStruct((rank, rank +...  80.8 us
    ppermute x14, waiting for transfers between devices, swap(): return lax.ppermute(value, AXES, [(i, i ^ bit) for i in range(size)])  23 us
    pallas_call x1, Pallas kernels, local_grams(): pl.pallas_call(functools.partial(gram_kernel, scale), grid=(columns // ti...  19.4 us
    ppermute x14, starting transfers between devices, swap(): return lax.ppermute(value, AXES, [(i, i ^ bit) for i in range(size)])  16.4 us
    pallas_call x1, Pallas kernels, apply_mix(): pl.pallas_call(apply_kernel, grid=(columns // tile,), in_specs=[pl.BlockS...  13.3 us
    unnamed x5, local copies, waits for them, and re-layouts  3.48 us
  transfers between devices with their start and end apart: 14, of which 8 were waited for; matrix products, arithmetic and copies ran while one was open for 0% of the time, Pallas kernels for 0%

profile of v1, /device:TPU:0, one launch (start us, length us, event | category | flops | bytes accessed | tf_op | source)
XLA Modules:
  0.0 157.6 jit_solution(2392152315152188325)
XLA Ops:
  0.6 0.0 copy-start
  0.6 2.2 %copy-done = f32[128,8192]{1,0:T(8,128)S(1)} copy-done((f32[128,8192]{1,0:T(8,128)S(1)}, f32[128,8192]{1,0:T(8,128)}, u32[]{:S(2)}) %copy-start) | copy-done | bytes 4194328
  2.8 19.4 %grams.1 = f32[1504,128]{1,0:T(8,128)S(1)} custom-call(f32[256,8192]{1,0:T(8,128)} %modes_ref.3, f32[3,64,8192]{2,1,0:T(8,128)} %snaps_ref.3, f32[128,8192]{1,0:T(8,128)S(1)} %copy-done), custom_call_target="tpu_custom_call" | custom-call | tf_op jit(solution)/shard_map/grams/pallas_call | solution.py:200
  22.2 0.0 copy-start.1
  22.2 0.5 collective-permute-start
  22.8 1.3 collective-permute-done
  24.1 0.1 select_add_fusion
  24.2 2.9 %collective-permute-start.1 = (f32[256,128]{1,0:T(8,128)S(1)}, f32[256,128]{1,0:T(8,128)S(1)}, u32[]{:S(2)}, u32[]{:S(2)}) collective-permute-start(f32[256,128]{1,0:T(8,128)S(1)} %get-tuple-element.16), channel_id=1, source_target_pairs={{0,2},{1,3},{2,0},{3,1},{4,6},{5,7},{6,4},{7,5},{8,10},{9,11},{10,... | collective-permute-start | bytes 393224 | tf_op jit(solution)/shard_map/ppermute | solution.py:221
  27.1 1.5 collective-permute-start.5
  28.7 1.6 %collective-permute-start.9 = (f32[240,128]{1,0:T(8,128)S(1)}, f32[240,128]{1,0:T(8,128)S(1)}, u32[]{:S(2)}, u32[]{:S(2)}) collective-permute-start(f32[240,128]{1,0:T(8,128)S(1)} %slice.24), channel_id=1, source_target_pairs={{0,8},{1,9},{2,10},{3,11},{4,12},{5,13},{6,14},{7,15},{8,0},{9,1},... | collective-permute-start | bytes 368648 | tf_op jit(solution)/shard_map/ppermute | solution.py:221
  30.3 0.6 collective-permute-done.1
  30.9 1.5 collective-permute-done.5
  32.4 1.6 %collective-permute-start.2 = (f32[256,128]{1,0:T(8,128)S(1)}, f32[256,128]{1,0:T(8,128)S(1)}, u32[]{:S(2)}, u32[]{:S(2)}) collective-permute-start(f32[256,128]{1,0:T(8,128)S(1)} %get-tuple-element.14), channel_id=1, source_target_pairs={{0,4},{1,5},{2,6},{3,7},{4,0},{5,1},{6,2},{7,3},{8,12},{9,13},{10,... | collective-permute-start | bytes 393224 | tf_op jit(solution)/shard_map/ppermute | solution.py:221
  34.0 1.6 collective-permute-start.6
  35.6 0.0 collective-permute-done.9
  35.6 2.7 %collective-permute-start.10 = (f32[240,128]{1,0:T(8,128)S(1)}, f32[240,128]{1,0:T(8,128)S(1)}, u32[]{:S(2)}, u32[]{:S(2)}) collective-permute-start(f32[240,128]{1,0:T(8,128)S(1)} %slice_add_fusion), channel_id=1, source_target_pairs={{0,16},{1,17},{2,18},{3,19},{4,20},{5,21},{6,22},{7,23},{8,24},{9,... | collective-permute-start | bytes 368648 | tf_op jit(solution)/shard_map/ppermute | solution.py:221
  38.3 0.0 collective-permute-done.2
  38.3 0.8 collective-permute-start.3
  39.1 4.9 %collective-permute-done.6 = f32[256,128]{1,0:T(8,128)S(1)} collective-permute-done((f32[256,128]{1,0:T(8,128)S(1)}, f32[256,128]{1,0:T(8,128)S(1)}, u32[]{:S(2)}, u32[]{:S(2)}) %collective-permute-start.6) | collective-permute-done | bytes 131104 | tf_op jit(solution)/shard_map/ppermute | solution.py:221
  44.0 0.1 collective-permute-start.7
  44.1 0.0 collective-permute-done.10
  44.1 0.4 collective-permute-start.11
  44.6 1.3 collective-permute-done.3
  45.9 1.8 %collective-permute-start.4 = (f32[256,128]{1,0:T(8,128)S(1)}, f32[256,128]{1,0:T(8,128)S(1)}, u32[]{:S(2)}, u32[]{:S(2)}) collective-permute-start(f32[256,128]{1,0:T(8,128)S(1)} %add.46), channel_id=1, source_target_pairs={{0,16},{1,17},{2,18},{3,19},{4,20},{5,21},{6,22},{7,23},{8,24},{9,... | collective-permute-start | bytes 393224 | tf_op jit(solution)/shard_map/ppermute | solution.py:221
  47.7 6.9 %collective-permute-done.7 = f32[256,128]{1,0:T(8,128)S(1)} collective-permute-done((f32[256,128]{1,0:T(8,128)S(1)}, f32[256,128]{1,0:T(8,128)S(1)}, u32[]{:S(2)}, u32[]{:S(2)}) %collective-permute-start.7) | collective-permute-done | bytes 131104 | tf_op jit(solution)/shard_map/ppermute | solution.py:221
  54.6 0.6 collective-permute-start.8
  55.2 0.0 collective-permute-done.11
  55.2 0.1 collective-permute-start.12
  55.3 4.9 %collective-permute-done.12 = f32[240,128]{1,0:T(8,128)S(1)} collective-permute-done((f32[240,128]{1,0:T(8,128)S(1)}, f32[240,128]{1,0:T(8,128)S(1)}, u32[]{:S(2)}, u32[]{:S(2)}) %collective-permute-start.12) | collective-permute-done | bytes 122912 | tf_op jit(solution)/shard_map/ppermute | solution.py:221
  60.2 0.0 collective-permute-done.4
  60.2 0.0 collective-permute-done.8
  60.3 0.1 collective-permute-start.13
  60.4 1.7 %collective-permute-done.13 = f32[752,128]{1,0:T(8,128)S(1)} collective-permute-done((f32[752,128]{1,0:T(8,128)S(1)}, f32[752,128]{1,0:T(8,128)S(1)}, u32[]{:S(2)}, u32[]{:S(2)}) %collective-permute-start.13) | collective-permute-done | bytes 385056 | tf_op jit(solution)/shard_map/ppermute | solution.py:221
  62.1 0.1 broadcast_select_fusion.1
  62.1 0.1 pad_maximum_fusion.packed_ref
  62.2 0.0 copy-done.1
  62.2 80.8 %core_updates.1 = (f32[256,448]{1,0:T(8,128)S(1)}, f32[256,256]{1,0:T(8,128)}, f32[3,256,320]{2,1,0:T(8,128)S(1)}) custom-call(f32[1504,128]{1,0:T(8,128)S(1)} %pad_maximum_fusion.packed_ref, f32[256,256]{1,0:T(8,128)S(1)} %copy-done.1), custom_call_target="tpu_custom_call" | custom-call | tf_op jit(solution)/shard_map/core_updates/pallas_call | solution.py:351
  143.0 1.3 copy.7
  144.3 13.3 %new_basis.1 = f32[256,8192]{1,0:T(8,128)} custom-call(f32[256,448]{1,0:T(8,128)S(1)} %get-tuple-element.6.mix_ref, f32[256,8192]{1,0:T(8,128)} %modes_ref.3, f32[3,64,8192]{2,1,0:T(8,128)} %snaps_ref.3), custom_call_target="tpu_custom_call" | custom-call | tf_op jit(solution)/shard_map/new_basis/pallas_call | solution.py:388
  (15 shorter events, 0.3 us)
Async XLA Ops:
  0.6 2.2 %copy-start = (f32[128,8192]{1,0:T(8,128)S(1)}, f32[128,8192]{1,0:T(8,128)}, u32[]{:S(2)}) copy-start(f32[128,8192]{1,0:T(8,128)} %probes_ref.1) | copy-start | bytes 12582916
  22.2 40.0 %copy-start.1 = (f32[256,256]{1,0:T(8,128)S(1)}, f32[256,256]{1,0:T(8,128)}, u32[]{:S(2)}) copy-start(f32[256,256]{1,0:T(8,128)} %core_ref.1) | copy-start | bytes 786436
  22.2 1.9 %collective-permute-start = (f32[752,128]{1,0:T(8,128)S(1)}, f32[752,128]{1,0:T(8,128)S(1)}, u32[]{:S(2)}, u32[]{:S(2)}) collective-permute-start(f32[752,128]{1,0:T(8,128)S(1)} %slice_select_fusion), channel_id=1, source_target_pairs={{0,1},{1,0},{2,3},{3,2},{4,5},{5,4},{6,7},{7,6},{8,9},{9,8},{10,11... | collective-permute-start | bytes 1155080 | tf_op jit(solution)/shard_map/ppermute | solution.py:221
  24.2 6.7 %collective-permute-start.1 = (f32[256,128]{1,0:T(8,128)S(1)}, f32[256,128]{1,0:T(8,128)S(1)}, u32[]{:S(2)}, u32[]{:S(2)}) collective-permute-start(f32[256,128]{1,0:T(8,128)S(1)} %get-tuple-element.16), channel_id=1, source_target_pairs={{0,2},{1,3},{2,0},{3,1},{4,6},{5,7},{6,4},{7,5},{8,10},{9,11},{10,... | collective-permute-start | bytes 393224 | tf_op jit(solution)/shard_map/ppermute | solution.py:221
  27.1 5.3 %collective-permute-start.5 = (f32[256,128]{1,0:T(8,128)S(1)}, f32[256,128]{1,0:T(8,128)S(1)}, u32[]{:S(2)}, u32[]{:S(2)}) collective-permute-start(f32[256,128]{1,0:T(8,128)S(1)} %get-tuple-element.17), channel_id=1, source_target_pairs={{0,4},{1,5},{2,6},{3,7},{4,0},{5,1},{6,2},{7,3},{8,12},{9,13},{10,... | collective-permute-start | bytes 393224 | tf_op jit(solution)/shard_map/ppermute | solution.py:221
  28.7 6.9 %collective-permute-start.9 = (f32[240,128]{1,0:T(8,128)S(1)}, f32[240,128]{1,0:T(8,128)S(1)}, u32[]{:S(2)}, u32[]{:S(2)}) collective-permute-start(f32[240,128]{1,0:T(8,128)S(1)} %slice.24), channel_id=1, source_target_pairs={{0,8},{1,9},{2,10},{3,11},{4,12},{5,13},{6,14},{7,15},{8,0},{9,1},... | collective-permute-start | bytes 368648 | tf_op jit(solution)/shard_map/ppermute | solution.py:221
  32.4 5.9 %collective-permute-start.2 = (f32[256,128]{1,0:T(8,128)S(1)}, f32[256,128]{1,0:T(8,128)S(1)}, u32[]{:S(2)}, u32[]{:S(2)}) collective-permute-start(f32[256,128]{1,0:T(8,128)S(1)} %get-tuple-element.14), channel_id=1, source_target_pairs={{0,4},{1,5},{2,6},{3,7},{4,0},{5,1},{6,2},{7,3},{8,12},{9,13},{10,... | collective-permute-start | bytes 393224 | tf_op jit(solution)/shard_map/ppermute | solution.py:221
  34.0 10.0 %collective-permute-start.6 = (f32[256,128]{1,0:T(8,128)S(1)}, f32[256,128]{1,0:T(8,128)S(1)}, u32[]{:S(2)}, u32[]{:S(2)}) collective-permute-start(f32[256,128]{1,0:T(8,128)S(1)} %get-tuple-element.15), channel_id=1, source_target_pairs={{0,8},{1,9},{2,10},{3,11},{4,12},{5,13},{6,14},{7,15},{8,0},{9,1},... | collective-permute-start | bytes 393224 | tf_op jit(solution)/shard_map/ppermute | solution.py:221
  35.6 8.5 %collective-permute-start.10 = (f32[240,128]{1,0:T(8,128)S(1)}, f32[240,128]{1,0:T(8,128)S(1)}, u32[]{:S(2)}, u32[]{:S(2)}) collective-permute-start(f32[240,128]{1,0:T(8,128)S(1)} %slice_add_fusion), channel_id=1, source_target_pairs={{0,16},{1,17},{2,18},{3,19},{4,20},{5,21},{6,22},{7,23},{8,24},{9,... | collective-permute-start | bytes 368648 | tf_op jit(solution)/shard_map/ppermute | solution.py:221
  38.3 7.5 %collective-permute-start.3 = (f32[256,128]{1,0:T(8,128)S(1)}, f32[256,128]{1,0:T(8,128)S(1)}, u32[]{:S(2)}, u32[]{:S(2)}) collective-permute-start(f32[256,128]{1,0:T(8,128)S(1)} %add.45), channel_id=1, source_target_pairs={{0,8},{1,9},{2,10},{3,11},{4,12},{5,13},{6,14},{7,15},{8,0},{9,1},... | collective-permute-start | bytes 393224 | tf_op jit(solution)/shard_map/ppermute | solution.py:221
  44.0 10.5 %collective-permute-start.7 = (f32[256,128]{1,0:T(8,128)S(1)}, f32[256,128]{1,0:T(8,128)S(1)}, u32[]{:S(2)}, u32[]{:S(2)}) collective-permute-start(f32[256,128]{1,0:T(8,128)S(1)} %add.49), channel_id=1, source_target_pairs={{0,16},{1,17},{2,18},{3,19},{4,20},{5,21},{6,22},{7,23},{8,24},{9,... | collective-permute-start | bytes 393224 | tf_op jit(solution)/shard_map/ppermute | solution.py:221
  44.1 11.1 %collective-permute-start.11 = (f32[240,128]{1,0:T(8,128)S(1)}, f32[240,128]{1,0:T(8,128)S(1)}, u32[]{:S(2)}, u32[]{:S(2)}) collective-permute-start(f32[240,128]{1,0:T(8,128)S(1)} %add.53), channel_id=1, source_target_pairs={{0,2},{1,3},{2,0},{3,1},{4,6},{5,7},{6,4},{7,5},{8,10},{9,11},{10,... | collective-permute-start | bytes 368648 | tf_op jit(solution)/shard_map/ppermute | solution.py:221
  45.9 14.3 %collective-permute-start.4 = (f32[256,128]{1,0:T(8,128)S(1)}, f32[256,128]{1,0:T(8,128)S(1)}, u32[]{:S(2)}, u32[]{:S(2)}) collective-permute-start(f32[256,128]{1,0:T(8,128)S(1)} %add.46), channel_id=1, source_target_pairs={{0,16},{1,17},{2,18},{3,19},{4,20},{5,21},{6,22},{7,23},{8,24},{9,... | collective-permute-start | bytes 393224 | tf_op jit(solution)/shard_map/ppermute | solution.py:221
  54.6 5.7 %collective-permute-start.8 = (f32[256,128]{1,0:T(8,128)S(1)}, f32[256,128]{1,0:T(8,128)S(1)}, u32[]{:S(2)}, u32[]{:S(2)}) collective-permute-start(f32[256,128]{1,0:T(8,128)S(1)} %add.50), channel_id=1, source_target_pairs={{0,2},{1,3},{2,0},{3,1},{4,6},{5,7},{6,4},{7,5},{8,10},{9,11},{10,... | collective-permute-start | bytes 393224 | tf_op jit(solution)/shard_map/ppermute | solution.py:221
  55.2 4.9 %collective-permute-start.12 = (f32[240,128]{1,0:T(8,128)S(1)}, f32[240,128]{1,0:T(8,128)S(1)}, u32[]{:S(2)}, u32[]{:S(2)}) collective-permute-start(f32[240,128]{1,0:T(8,128)S(1)} %add.54), channel_id=1, source_target_pairs={{0,4},{1,5},{2,6},{3,7},{4,0},{5,1},{6,2},{7,3},{8,12},{9,13},{10,... | collective-permute-start | bytes 368648 | tf_op jit(solution)/shard_map/ppermute | solution.py:221
  60.3 1.8 %collective-permute-start.13 = (f32[752,128]{1,0:T(8,128)S(1)}, f32[752,128]{1,0:T(8,128)S(1)}, u32[]{:S(2)}, u32[]{:S(2)}) collective-permute-start(f32[752,128]{1,0:T(8,128)S(1)} %pad_maximum_fusion.1), channel_id=1, source_target_pairs={{0,1},{1,0},{2,3},{3,2},{4,5},{5,4},{6,7},{7,6},{8,9},{9,8},{10,11... | collective-permute-start | bytes 1155080 | tf_op jit(solution)/shard_map/ppermute | solution.py:221

commit v2 on v1

--- a/solution.py
+++ b/solution.py
@@ -12,7 +12,8 @@
 FULL = lax.Precision.HIGHEST
 LANES = 128
 GROUP = 8
-PANEL = 64
+PANEL = 32
+FINAL_PANEL = 64
 
 
 def nn(left, right):
@@ -37,70 +38,94 @@
     return jnp.concatenate([column] * (order // LANES), axis=1)
 
 
-def inverse_factor(matrix):
-    order = matrix.shape[0]
+def eliminate_panel(block, start, inverting):
+    size, order = block.shape
     lane = lax.broadcasted_iota(jnp.int32, (GROUP, order), 1)
     row = lax.broadcasted_iota(jnp.int32, (GROUP, order), 0)
     row_one = lax.broadcasted_iota(jnp.int32, (GROUP, LANES), 0)
-    finished = []
-    groups = PANEL // GROUP
-    for start in range(0, order, PANEL):
-        finish = start + PANEL
-        held = [matrix[g * GROUP:(g + 1) * GROUP, :] for g in range(groups)]
-        panel = []
-        for g0 in range(groups):
-            first = start + g0 * GROUP
-            spread = [
-                [
-                    jnp.broadcast_to(held[g][:, first + j:first + j + 1], (GROUP, LANES))
-                    for g in range(g0, groups)
-                ]
-                for j in range(GROUP)
+    groups = size // GROUP
+    held = [block[g * GROUP:(g + 1) * GROUP, :] for g in range(groups)]
+    panel = []
+
+    def spread(first, g0):
+        return [
+            [
+                jnp.broadcast_to(held[g][:, first + j:first + j + 1], (GROUP, LANES))
+                for g in range(g0, groups)
             ]
+            for j in range(GROUP)
+        ]
+
+    own = spread(start, 0)
+    for g0 in range(groups):
+        first = start + g0 * GROUP
+        ahead = spread(first + GROUP, g0) if g0 + 1 < groups else []
+        if inverting:
             inside = (lane >= first) & (lane < first + GROUP)
             held[g0] = jnp.where(inside, jnp.where(lane - first == row, 1.0, 0.0), held[g0])
             for g in range(g0 + 1, groups):
                 held[g] = jnp.where(inside, 0.0, held[g])
-            pivot_column = jnp.ones((GROUP, LANES), jnp.float32)
-            factors = []
-            for j in range(GROUP):
-                pivot = jnp.broadcast_to(spread[j][0][j:j + 1, :], (GROUP, LANES))
-                inverse = pltpu.reciprocal(pivot, approx=True)
-                inverse = inverse * (2.0 - pivot * inverse)
-                pivot_column = jnp.where(row_one == j, pivot, pivot_column)
-                factor = [block * inverse for block in spread[j]]
-                for later in range(j + 1, GROUP):
-                    across = jnp.broadcast_to(spread[later][0][j:j + 1, :], (GROUP, LANES))
-                    for t in range(groups - g0):
-                        spread[later][t] = spread[later][t] - factor[t] * across
-                factor[0] = jnp.where(row_one > j, factor[0], 0.0)
-                factors.append(factor)
-            for j in range(GROUP):
-                pivot_row = jnp.broadcast_to(held[g0][j:j + 1, :], (GROUP, order))
+        pivot_column = jnp.ones((GROUP, LANES), jnp.float32)
+        factors = []
+        for j in range(GROUP):
+            pivot = jnp.broadcast_to(own[j][0][j:j + 1, :], (GROUP, LANES))
+            inverse = pltpu.reciprocal(pivot, approx=True)
+            pivot_column = jnp.where(row_one == j, pivot, pivot_column)
+            factor = [column * inverse for column in own[j]]
+            for column in own[j + 1:] + ahead:
+                across = jnp.broadcast_to(column[0][j:j + 1, :], (GROUP, LANES))
                 for t in range(groups - g0):
-                    held[g0 + t] = held[g0 + t] - wide(factors[j][t], order) * pivot_row
-            panel.append(held[g0] * wide(lax.rsqrt(pivot_column), order))
-        finished.extend(panel)
-        if finish < order:
-            scaled = jnp.concatenate(
-                [
-                    jnp.where((lane >= start + GROUP * (g + 1)) & (lane < finish), 0.0, panel[g])
-                    for g in range(groups)
-                ],
-                axis=0,
-            )
+                    column[t] = column[t] - factor[t] * across
+            factor[0] = jnp.where(row_one > j, factor[0], 0.0)
+            factors.append(factor)
+        for j in range(GROUP):
+            pivot_row = jnp.broadcast_to(held[g0][j:j + 1, :], (GROUP, order))
+            for t in range(groups - g0):
+                held[g0 + t] = held[g0 + t] - wide(factors[j][t], order) * pivot_row
+        panel.append(held[g0] * wide(lax.rsqrt(pivot_column), order))
+        own = [column[1:] for column in ahead]
+        yield
+    if inverting:
+        panel = [
+            jnp.where((lane >= start + GROUP * (g + 1)) & (lane < start + size), 0.0, panel[g])
+            for g in range(groups)
+        ]
+    return jnp.concatenate(panel, axis=0)
+
+
+def finish(steps):
+    while True:
+        try:
+            next(steps)
+        except StopIteration as done:
+            return done.value
+
+
+def stacked_square(panel, begin):
+    high = panel.astype(jnp.bfloat16)
+    left = panel - high.astype(jnp.float32)
+    mid = left.astype(jnp.bfloat16)
+    low = (left - mid.astype(jnp.float32)).astype(jnp.bfloat16)
+    first = jnp.concatenate([high, high, mid, mid, high, low], axis=0)
+    second = jnp.concatenate([high, mid, high, mid, low, high], axis=0)
+    return lax.dot_general(
+        first[:, begin:], second, (((0,), (0,)), ((), ())), preferred_element_type=jnp.float32
+    )
+
+
+def inverse_factor(matrix):
+    order = matrix.shape[0]
+    finished = []
+    for start in range(0, order, PANEL):
+        end = start + PANEL
+        panel = finish(eliminate_panel(matrix[:PANEL, :], start, True))
+        finished.append(panel)
+        if end < order:
             rest = matrix[PANEL:, :]
             rest_lane = lax.broadcasted_iota(jnp.int32, rest.shape, 1)
-            rest = jnp.where((rest_lane >= start) & (rest_lane < finish), 0.0, rest)
-            matrix = rest - tn(scaled[:, finish:], scaled)
+            rest = jnp.where((rest_lane >= start) & (rest_lane < end), 0.0, rest)
+            matrix = rest - stacked_square(panel, end)
     lowered = jnp.concatenate(finished, axis=0)
-    lane = lax.broadcasted_iota(jnp.int32, lowered.shape, 1)
-    row = lax.broadcasted_iota(jnp.int32, lowered.shape, 0)
-    return jnp.where(lane <= row, lowered, 0.0)
-
-
-def lower_factor(matrix):
-    lowered = nt(matrix, inverse_factor(matrix))
     lane = lax.broadcasted_iota(jnp.int32, lowered.shape, 1)
     row = lax.broadcasted_iota(jnp.int32, lowered.shape, 0)
     return jnp.where(lane <= row, lowered, 0.0)
@@ -255,7 +280,7 @@
 
 
 def core_kernel(
-    packed_ref, core_ref, mix_ref, core_out, captured_ref, energy_ref, norms_ref, inner_ref, snaps_ref, kept_ref
+    packed_ref, core_ref, mix_ref, energy_out, captured_ref, energy_ref, norms_ref, inner_ref, snaps_ref, kept_ref
 ):
     rank = core_ref.shape[0]
     batches = captured_ref.shape[0]
@@ -341,7 +366,7 @@
         + [kept_ref[:, rank + b * LANES:rank + b * LANES + width] for b in range(batches)],
         axis=1,
     )
-    core_out[...] = lower_factor(energy_ref[...])
+    energy_out[...] = energy_ref[...]
 
 
 def small_algebra(packed, core, batches, width, probes):
@@ -367,37 +392,78 @@
     )(packed, core)
 
 
-def apply_kernel(mix_ref, modes_ref, snaps_ref, out_ref):
+def apply_kernel(mix_ref, energy_ref, modes_ref, snaps_ref, out_ref, core_ref, mixed_ref, left_ref):
+    step = pl.program_id(0)
     count, width, columns = snaps_ref.shape
-    rows = jnp.concatenate([modes_ref[...], snaps_ref[...].reshape(count * width, columns)], axis=0)
-    high, low = split(rows)
-    mix_high, mix_low = split(mix_ref[...])
+    rank = energy_ref.shape[0]
+
+    @pl.when(step == 0)
+    def _():
+        left_ref[...] = energy_ref[...]
+        high, low = split(mix_ref[...])
+        mixed_ref[0] = high
+        mixed_ref[1] = low
 
     def one(left, right):
         return lax.dot_general(
             left, right, (((1,), (0,)), ((), ())), preferred_element_type=jnp.float32
         )
 
-    out_ref[...] = one(mix_high, high) + (one(mix_high, low) + one(mix_low, high))
-
-
-def apply_mix(mix, modes, snaps):
+    def block_of(start):
+        end = start + FINAL_PANEL
+        steps = eliminate_panel(left_ref[start:end, :], start, False)
+        piece = columns // (FINAL_PANEL // GROUP)
+        for number in range(FINAL_PANEL // GROUP):
+            part = slice(number * piece, (number + 1) * piece)
+            rows = jnp.concatenate(
+                [modes_ref[:, part], snaps_ref[:, :, part].reshape(count * width, piece)], axis=0
+            )
+            high, low = split(rows)
+            mix_high, mix_low = mixed_ref[0], mixed_ref[1]
+            out_ref[:, part] = one(mix_high, high) + (one(mix_high, low) + one(mix_low, high))
+            next(steps)
+        panel = finish(steps)
+        left_ref[start:end, :] = panel
+        if end < rank:
+            left_ref[end:, :] = left_ref[end:, :] - tn(panel[:, end:], panel)
+        else:
+            lane = lax.broadcasted_iota(jnp.int32, (rank, rank), 1)
+            row = lax.broadcasted_iota(jnp.int32, (rank, rank), 0)
+            core_ref[...] = jnp.where(lane >= row, left_ref[...], 0.0).T
+
+    for number in range(rank // FINAL_PANEL):
+        pl.when(step == number)(functools.partial(block_of, number * FINAL_PANEL))
+
+
+def apply_mix(mix, energy, modes, snaps):
     rank, columns = modes.shape
     count, width, _ = snaps.shape
-    tile = 1024
+    steps = rank // FINAL_PANEL
+    tile = columns // steps
     return pl.pallas_call(
         apply_kernel,
-        grid=(columns // tile,),
+        grid=(steps,),
         in_specs=[
             pl.BlockSpec(mix.shape, lambda i: (0, 0)),
+            pl.BlockSpec(energy.shape, lambda i: (0, 0)),
             pl.BlockSpec((rank, tile), lambda i: (0, i)),
             pl.BlockSpec((count, width, tile), lambda i: (0, 0, i)),
         ],
-        out_specs=pl.BlockSpec((rank, tile), lambda i: (0, i)),
-        out_shape=jax.ShapeDtypeStruct((rank, columns), jnp.float32),
+        out_specs=[
+            pl.BlockSpec((rank, tile), lambda i: (0, i)),
+            pl.BlockSpec((rank, rank), lambda i: (0, 0)),
+        ],
+        out_shape=[
+            jax.ShapeDtypeStruct((rank, columns), jnp.float32),
+            jax.ShapeDtypeStruct((rank, rank), jnp.float32),
+        ],
+        scratch_shapes=[
+            pltpu.VMEM((2,) + mix.shape, jnp.bfloat16),
+            pltpu.VMEM((rank, rank), jnp.float32),
+        ],
         compiler_params=pltpu.CompilerParams(vmem_limit_bytes=48 << 20),
         name="new_basis",
-    )(mix, modes, snaps)
+    )(mix, energy, modes, snaps)
 
 
 def body(modes, snaps, probes, core, *, devices):
@@ -405,8 +471,9 @@
     batches, width, _ = snaps.shape
     scale = 1.0 / (columns * devices)
     packed = sum_over_devices(local_grams(modes, snaps, probes, scale), devices)
-    mix, new_core, captured = small_algebra(packed, core, batches, width, probes.shape[0])
-    return apply_mix(mix, modes, snaps), new_core, captured
+    mix, energy, captured = small_algebra(packed, core, batches, width, probes.shape[0])
+    new_modes, new_core = apply_mix(mix, energy, modes, snaps)
+    return new_modes, new_core, captured
 
 
 def solution(mesh):

time: 158 us -> 134 us (0.85)
  Pallas kernels: 113 us -> 90.1 us
    pallas_call x1, Pallas kernels: 80.8 us -> 55.8 us  [small_algebra(): pl.pallas_call(core_kernel, out_shape=[jax.ShapeDtypeStruct((rank, rank +...]
    pallas_call x1, Pallas kernels: 13.3 us -> 14.9 us  [apply_mix(): pl.pallas_call(apply_kernel, grid=(steps,), in_specs=[pl.BlockSpec(mix.sh...]
where the time goes in v2:
time: 134 us
  Pallas kernels  90.1 us (67%)
  waiting for transfers between devices  23 us (17%)
  starting transfers between devices  16.4 us (12%)
  local copies, waits for them, and re-layouts  3.51 us (3%)
    pallas_call x1, Pallas kernels, small_algebra(): pl.pallas_call(core_kernel, out_shape=[jax.ShapeDtypeStruct((rank, rank +...  55.8 us
    ppermute x14, waiting for transfers between devices, swap(): return lax.ppermute(value, AXES, [(i, i ^ bit) for i in range(size)])  23 us
    pallas_call x1, Pallas kernels, local_grams(): pl.pallas_call(functools.partial(gram_kernel, scale), grid=(columns // ti...  19.4 us
    ppermute x14, starting transfers between devices, swap(): return lax.ppermute(value, AXES, [(i, i ^ bit) for i in range(size)])  16.4 us
    pallas_call x1, Pallas kernels, apply_mix(): pl.pallas_call(apply_kernel, grid=(steps,), in_specs=[pl.BlockSpec(mix.sh...  14.9 us
    unnamed x5, local copies, waits for them, and re-layouts  3.49 us
  transfers between devices with their start and end apart: 14, of which 8 were waited for; matrix products, arithmetic and copies ran while one was open for 0% of the time, Pallas kernels for 0%

profile of v2, /device:TPU:0, one launch (start us, length us, event | category | flops | bytes accessed | tf_op | source)
XLA Modules:
  0.0 134.3 jit_solution(5416385789395516353)
XLA Ops:
  0.6 0.0 copy-start
  0.6 2.2 %copy-done = f32[128,8192]{1,0:T(8,128)S(1)} copy-done((f32[128,8192]{1,0:T(8,128)S(1)}, f32[128,8192]{1,0:T(8,128)}, u32[]{:S(2)}) %copy-start) | copy-done | bytes 4194328
  2.8 19.4 %grams.1 = f32[1504,128]{1,0:T(8,128)S(1)} custom-call(f32[256,8192]{1,0:T(8,128)} %modes_ref.3, f32[3,64,8192]{2,1,0:T(8,128)} %snaps_ref.3, f32[128,8192]{1,0:T(8,128)S(1)} %copy-done), custom_call_target="tpu_custom_call" | custom-call | tf_op jit(solution)/shard_map/grams/pallas_call | solution.py:225
  22.2 0.0 copy-start.1
  22.2 0.5 collective-permute-start
  22.8 1.3 collective-permute-done
  24.1 0.1 select_add_fusion
  24.2 2.9 %collective-permute-start.1 = (f32[256,128]{1,0:T(8,128)S(1)}, f32[256,128]{1,0:T(8,128)S(1)}, u32[]{:S(2)}, u32[]{:S(2)}) collective-permute-start(f32[256,128]{1,0:T(8,128)S(1)} %get-tuple-element.20), channel_id=1, source_target_pairs={{0,2},{1,3},{2,0},{3,1},{4,6},{5,7},{6,4},{7,5},{8,10},{9,11},{10,... | collective-permute-start | bytes 393224 | tf_op jit(solution)/shard_map/ppermute | solution.py:246
  27.1 1.5 %collective-permute-start.5 = (f32[256,128]{1,0:T(8,128)S(1)}, f32[256,128]{1,0:T(8,128)S(1)}, u32[]{:S(2)}, u32[]{:S(2)}) collective-permute-start(f32[256,128]{1,0:T(8,128)S(1)} %get-tuple-element.21), channel_id=1, source_target_pairs={{0,4},{1,5},{2,6},{3,7},{4,0},{5,1},{6,2},{7,3},{8,12},{9,13},{10,... | collective-permute-start | bytes 393224 | tf_op jit(solution)/shard_map/ppermute | solution.py:246
  28.7 1.6 %collective-permute-start.9 = (f32[240,128]{1,0:T(8,128)S(1)}, f32[240,128]{1,0:T(8,128)S(1)}, u32[]{:S(2)}, u32[]{:S(2)}) collective-permute-start(f32[240,128]{1,0:T(8,128)S(1)} %slice.24), channel_id=1, source_target_pairs={{0,8},{1,9},{2,10},{3,11},{4,12},{5,13},{6,14},{7,15},{8,0},{9,1},... | collective-permute-start | bytes 368648 | tf_op jit(solution)/shard_map/ppermute | solution.py:246
  30.3 0.6 collective-permute-done.1
  30.9 1.5 %collective-permute-done.5 = f32[256,128]{1,0:T(8,128)S(1)} collective-permute-done((f32[256,128]{1,0:T(8,128)S(1)}, f32[256,128]{1,0:T(8,128)S(1)}, u32[]{:S(2)}, u32[]{:S(2)}) %collective-permute-start.5) | collective-permute-done | bytes 131104 | tf_op jit(solution)/shard_map/ppermute | solution.py:246
  32.4 1.6 %collective-permute-start.2 = (f32[256,128]{1,0:T(8,128)S(1)}, f32[256,128]{1,0:T(8,128)S(1)}, u32[]{:S(2)}, u32[]{:S(2)}) collective-permute-start(f32[256,128]{1,0:T(8,128)S(1)} %get-tuple-element.18), channel_id=1, source_target_pairs={{0,4},{1,5},{2,6},{3,7},{4,0},{5,1},{6,2},{7,3},{8,12},{9,13},{10,... | collective-permute-start | bytes 393224 | tf_op jit(solution)/shard_map/ppermute | solution.py:246
  34.0 1.6 %collective-permute-start.6 = (f32[256,128]{1,0:T(8,128)S(1)}, f32[256,128]{1,0:T(8,128)S(1)}, u32[]{:S(2)}, u32[]{:S(2)}) collective-permute-start(f32[256,128]{1,0:T(8,128)S(1)} %get-tuple-element.19), channel_id=1, source_target_pairs={{0,8},{1,9},{2,10},{3,11},{4,12},{5,13},{6,14},{7,15},{8,0},{9,1},... | collective-permute-start | bytes 393224 | tf_op jit(solution)/shard_map/ppermute | solution.py:246
  35.6 0.0 collective-permute-done.9
  35.6 2.7 %collective-permute-start.10 = (f32[240,128]{1,0:T(8,128)S(1)}, f32[240,128]{1,0:T(8,128)S(1)}, u32[]{:S(2)}, u32[]{:S(2)}) collective-permute-start(f32[240,128]{1,0:T(8,128)S(1)} %slice_add_fusion), channel_id=1, source_target_pairs={{0,16},{1,17},{2,18},{3,19},{4,20},{5,21},{6,22},{7,23},{8,24},{9,... | collective-permute-start | bytes 368648 | tf_op jit(solution)/shard_map/ppermute | solution.py:246
  38.3 0.0 collective-permute-done.2
  38.3 0.8 collective-permute-start.3
  39.1 4.9 %collective-permute-done.6 = f32[256,128]{1,0:T(8,128)S(1)} collective-permute-done((f32[256,128]{1,0:T(8,128)S(1)}, f32[256,128]{1,0:T(8,128)S(1)}, u32[]{:S(2)}, u32[]{:S(2)}) %collective-permute-start.6) | collective-permute-done | bytes 131104 | tf_op jit(solution)/shard_map/ppermute | solution.py:246
  44.0 0.1 collective-permute-start.7
  44.1 0.0 collective-permute-done.10
  44.1 0.4 collective-permute-start.11
  44.6 1.3 collective-permute-done.3
  45.9 1.8 %collective-permute-start.4 = (f32[256,128]{1,0:T(8,128)S(1)}, f32[256,128]{1,0:T(8,128)S(1)}, u32[]{:S(2)}, u32[]{:S(2)}) collective-permute-start(f32[256,128]{1,0:T(8,128)S(1)} %add.46), channel_id=1, source_target_pairs={{0,16},{1,17},{2,18},{3,19},{4,20},{5,21},{6,22},{7,23},{8,24},{9,... | collective-permute-start | bytes 393224 | tf_op jit(solution)/shard_map/ppermute | solution.py:246
  47.7 6.9 %collective-permute-done.7 = f32[256,128]{1,0:T(8,128)S(1)} collective-permute-done((f32[256,128]{1,0:T(8,128)S(1)}, f32[256,128]{1,0:T(8,128)S(1)}, u32[]{:S(2)}, u32[]{:S(2)}) %collective-permute-start.7) | collective-permute-done | bytes 131104 | tf_op jit(solution)/shard_map/ppermute | solution.py:246
  54.6 0.6 collective-permute-start.8
  55.2 0.0 collective-permute-done.11
  55.2 0.1 collective-permute-start.12
  55.3 4.9 %collective-permute-done.12 = f32[240,128]{1,0:T(8,128)S(1)} collective-permute-done((f32[240,128]{1,0:T(8,128)S(1)}, f32[240,128]{1,0:T(8,128)S(1)}, u32[]{:S(2)}, u32[]{:S(2)}) %collective-permute-start.12) | collective-permute-done | bytes 122912 | tf_op jit(solution)/shard_map/ppermute | solution.py:246
  60.2 0.0 collective-permute-done.4
  60.2 0.0 collective-permute-done.8
  60.3 0.1 collective-permute-start.13
  60.4 1.7 %collective-permute-done.13 = f32[752,128]{1,0:T(8,128)S(1)} collective-permute-done((f32[752,128]{1,0:T(8,128)S(1)}, f32[752,128]{1,0:T(8,128)S(1)}, u32[]{:S(2)}, u32[]{:S(2)}) %collective-permute-start.13) | collective-permute-done | bytes 385056 | tf_op jit(solution)/shard_map/ppermute | solution.py:246
  62.1 0.1 broadcast_select_fusion.1
  62.1 0.1 pad_maximum_fusion.packed_ref
  62.2 0.0 copy-done.1
  62.2 55.8 %core_updates.1 = (f32[256,448]{1,0:T(8,128)S(1)}, f32[256,256]{1,0:T(8,128)S(1)}, f32[3,256,320]{2,1,0:T(8,128)S(1)}) custom-call(f32[1504,128]{1,0:T(8,128)S(1)} %pad_maximum_fusion.packed_ref, f32[256,256]{1,0:T(8,128)S(1)} %copy-done.1), custom_call_target="tpu_custom_call" | custom-call | tf_op jit(solution)/shard_map/core_updates/pallas_call | solution.py:376
  118.0 1.3 copy.7
  119.3 14.9 %new_basis.1 = (f32[256,8192]{1,0:T(8,128)}, f32[256,256]{1,0:T(8,128)}) custom-call(f32[256,448]{1,0:T(8,128)S(1)} %get-tuple-element.8.mix_ref, f32[256,256]{1,0:T(8,128)S(1)} %get-tuple-element.9.energy_ref, f32[256,8192]{1,0:T(8,128)} %modes_ref.3, f32[3,64,8192]{2,1,0:T(8,128)} %snaps_ref.3), custom_call_target="tpu_custom_call" | custom-call | tf_op jit(solution)/shard_map/new_basis/pallas_call | solution.py:443
  (15 shorter events, 0.3 us)
Async XLA Ops:
  0.6 2.2 %copy-start = (f32[128,8192]{1,0:T(8,128)S(1)}, f32[128,8192]{1,0:T(8,128)}, u32[]{:S(2)}) copy-start(f32[128,8192]{1,0:T(8,128)} %probes_ref.1) | copy-start | bytes 12582916
  22.2 40.0 %copy-start.1 = (f32[256,256]{1,0:T(8,128)S(1)}, f32[256,256]{1,0:T(8,128)}, u32[]{:S(2)}) copy-start(f32[256,256]{1,0:T(8,128)} %core_ref.1) | copy-start | bytes 786436
  22.2 1.9 %collective-permute-start = (f32[752,128]{1,0:T(8,128)S(1)}, f32[752,128]{1,0:T(8,128)S(1)}, u32[]{:S(2)}, u32[]{:S(2)}) collective-permute-start(f32[752,128]{1,0:T(8,128)S(1)} %slice_select_fusion), channel_id=1, source_target_pairs={{0,1},{1,0},{2,3},{3,2},{4,5},{5,4},{6,7},{7,6},{8,9},{9,8},{10,11... | collective-permute-start | bytes 1155080 | tf_op jit(solution)/shard_map/ppermute | solution.py:246
  24.2 6.7 %collective-permute-start.1 = (f32[256,128]{1,0:T(8,128)S(1)}, f32[256,128]{1,0:T(8,128)S(1)}, u32[]{:S(2)}, u32[]{:S(2)}) collective-permute-start(f32[256,128]{1,0:T(8,128)S(1)} %get-tuple-element.20), channel_id=1, source_target_pairs={{0,2},{1,3},{2,0},{3,1},{4,6},{5,7},{6,4},{7,5},{8,10},{9,11},{10,... | collective-permute-start | bytes 393224 | tf_op jit(solution)/shard_map/ppermute | solution.py:246
  27.1 5.3 %collective-permute-start.5 = (f32[256,128]{1,0:T(8,128)S(1)}, f32[256,128]{1,0:T(8,128)S(1)}, u32[]{:S(2)}, u32[]{:S(2)}) collective-permute-start(f32[256,128]{1,0:T(8,128)S(1)} %get-tuple-element.21), channel_id=1, source_target_pairs={{0,4},{1,5},{2,6},{3,7},{4,0},{5,1},{6,2},{7,3},{8,12},{9,13},{10,... | collective-permute-start | bytes 393224 | tf_op jit(solution)/shard_map/ppermute | solution.py:246
  28.7 6.9 %collective-permute-start.9 = (f32[240,128]{1,0:T(8,128)S(1)}, f32[240,128]{1,0:T(8,128)S(1)}, u32[]{:S(2)}, u32[]{:S(2)}) collective-permute-start(f32[240,128]{1,0:T(8,128)S(1)} %slice.24), channel_id=1, source_target_pairs={{0,8},{1,9},{2,10},{3,11},{4,12},{5,13},{6,14},{7,15},{8,0},{9,1},... | collective-permute-start | bytes 368648 | tf_op jit(solution)/shard_map/ppermute | solution.py:246
  32.4 5.9 %collective-permute-start.2 = (f32[256,128]{1,0:T(8,128)S(1)}, f32[256,128]{1,0:T(8,128)S(1)}, u32[]{:S(2)}, u32[]{:S(2)}) collective-permute-start(f32[256,128]{1,0:T(8,128)S(1)} %get-tuple-element.18), channel_id=1, source_target_pairs={{0,4},{1,5},{2,6},{3,7},{4,0},{5,1},{6,2},{7,3},{8,12},{9,13},{10,... | collective-permute-start | bytes 393224 | tf_op jit(solution)/shard_map/ppermute | solution.py:246
  34.0 10.0 %collective-permute-start.6 = (f32[256,128]{1,0:T(8,128)S(1)}, f32[256,128]{1,0:T(8,128)S(1)}, u32[]{:S(2)}, u32[]{:S(2)}) collective-permute-start(f32[256,128]{1,0:T(8,128)S(1)} %get-tuple-element.19), channel_id=1, source_target_pairs={{0,8},{1,9},{2,10},{3,11},{4,12},{5,13},{6,14},{7,15},{8,0},{9,1},... | collective-permute-start | bytes 393224 | tf_op jit(solution)/shard_map/ppermute | solution.py:246
  35.6 8.5 %collective-permute-start.10 = (f32[240,128]{1,0:T(8,128)S(1)}, f32[240,128]{1,0:T(8,128)S(1)}, u32[]{:S(2)}, u32[]{:S(2)}) collective-permute-start(f32[240,128]{1,0:T(8,128)S(1)} %slice_add_fusion), channel_id=1, source_target_pairs={{0,16},{1,17},{2,18},{3,19},{4,20},{5,21},{6,22},{7,23},{8,24},{9,... | collective-permute-start | bytes 368648 | tf_op jit(solution)/shard_map/ppermute | solution.py:246
  38.3 7.5 %collective-permute-start.3 = (f32[256,128]{1,0:T(8,128)S(1)}, f32[256,128]{1,0:T(8,128)S(1)}, u32[]{:S(2)}, u32[]{:S(2)}) collective-permute-start(f32[256,128]{1,0:T(8,128)S(1)} %add.45), channel_id=1, source_target_pairs={{0,8},{1,9},{2,10},{3,11},{4,12},{5,13},{6,14},{7,15},{8,0},{9,1},... | collective-permute-start | bytes 393224 | tf_op jit(solution)/shard_map/ppermute | solution.py:246
  44.0 10.5 %collective-permute-start.7 = (f32[256,128]{1,0:T(8,128)S(1)}, f32[256,128]{1,0:T(8,128)S(1)}, u32[]{:S(2)}, u32[]{:S(2)}) collective-permute-start(f32[256,128]{1,0:T(8,128)S(1)} %add.49), channel_id=1, source_target_pairs={{0,16},{1,17},{2,18},{3,19},{4,20},{5,21},{6,22},{7,23},{8,24},{9,... | collective-permute-start | bytes 393224 | tf_op jit(solution)/shard_map/ppermute | solution.py:246
  44.1 11.1 %collective-permute-start.11 = (f32[240,128]{1,0:T(8,128)S(1)}, f32[240,128]{1,0:T(8,128)S(1)}, u32[]{:S(2)}, u32[]{:S(2)}) collective-permute-start(f32[240,128]{1,0:T(8,128)S(1)} %add.53), channel_id=1, source_target_pairs={{0,2},{1,3},{2,0},{3,1},{4,6},{5,7},{6,4},{7,5},{8,10},{9,11},{10,... | collective-permute-start | bytes 368648 | tf_op jit(solution)/shard_map/ppermute | solution.py:246
  45.9 14.3 %collective-permute-start.4 = (f32[256,128]{1,0:T(8,128)S(1)}, f32[256,128]{1,0:T(8,128)S(1)}, u32[]{:S(2)}, u32[]{:S(2)}) collective-permute-start(f32[256,128]{1,0:T(8,128)S(1)} %add.46), channel_id=1, source_target_pairs={{0,16},{1,17},{2,18},{3,19},{4,20},{5,21},{6,22},{7,23},{8,24},{9,... | collective-permute-start | bytes 393224 | tf_op jit(solution)/shard_map/ppermute | solution.py:246
  54.6 5.7 %collective-permute-start.8 = (f32[256,128]{1,0:T(8,128)S(1)}, f32[256,128]{1,0:T(8,128)S(1)}, u32[]{:S(2)}, u32[]{:S(2)}) collective-permute-start(f32[256,128]{1,0:T(8,128)S(1)} %add.50), channel_id=1, source_target_pairs={{0,2},{1,3},{2,0},{3,1},{4,6},{5,7},{6,4},{7,5},{8,10},{9,11},{10,... | collective-permute-start | bytes 393224 | tf_op jit(solution)/shard_map/ppermute | solution.py:246
  55.2 4.9 %collective-permute-start.12 = (f32[240,128]{1,0:T(8,128)S(1)}, f32[240,128]{1,0:T(8,128)S(1)}, u32[]{:S(2)}, u32[]{:S(2)}) collective-permute-start(f32[240,128]{1,0:T(8,128)S(1)} %add.54), channel_id=1, source_target_pairs={{0,4},{1,5},{2,6},{3,7},{4,0},{5,1},{6,2},{7,3},{8,12},{9,13},{10,... | collective-permute-start | bytes 368648 | tf_op jit(solution)/shard_map/ppermute | solution.py:246
  60.3 1.8 %collective-permute-start.13 = (f32[752,128]{1,0:T(8,128)S(1)}, f32[752,128]{1,0:T(8,128)S(1)}, u32[]{:S(2)}, u32[]{:S(2)}) collective-permute-start(f32[752,128]{1,0:T(8,128)S(1)} %pad_maximum_fusion.1), channel_id=1, source_target_pairs={{0,1},{1,0},{2,3},{3,2},{4,5},{5,4},{6,7},{7,6},{8,9},{9,8},{10,11... | collective-permute-start | bytes 1155080 | tf_op jit(solution)/shard_map/ppermute | solution.py:246

commit v3 on v2

--- a/solution.py
+++ b/solution.py
@@ -13,7 +13,6 @@
 LANES = 128
 GROUP = 8
 PANEL = 32
-FINAL_PANEL = 64
 
 
 def nn(left, right):
@@ -145,7 +144,8 @@
 
 def packed_rows(rank, snap_count, batches):
     own = 3 * (rank // 2)
-    return own + (rank + snap_count) * (batches - 1) + (rank + snap_count) // 2
+    rows = own + (rank + snap_count) * (batches - 1) + (rank + snap_count) // 2
+    return -(-rows // (8 * GROUP)) * (8 * GROUP)
 
 
 def fold(block):
@@ -164,62 +164,77 @@
     )
 
 
-def gram_kernel(scale, modes_ref, snaps_ref, probes_ref, packed_ref, modes_out, snaps_out):
+def gram_kernel(
+    scale, modes_ref, snaps_ref, probes_ref, packed_ref, norms_out, cross_out, past_snaps, past_probes, own_out, own_cross, others_out
+):
     step = pl.program_id(0)
+    sums = (norms_out, cross_out, past_snaps, past_probes, own_out, own_cross, others_out)
 
     @pl.when(step == 0)
     def _():
-        modes_out[...] = jnp.zeros_like(modes_out)
-        snaps_out[...] = jnp.zeros_like(snaps_out)
-
-    count, width, columns = snaps_ref.shape
+        for ref in sums:
+            ref[...] = jnp.zeros_like(ref)
+
+    rank, columns = modes_ref.shape
+    count, width, _ = snaps_ref.shape
+    snap_count = count * width
     probe_count = probes_ref.shape[0]
-    spare = LANES - width
-    pieces = []
-    for batch in range(count):
-        pieces.append(snaps_ref[batch])
-        taken = min(max(probe_count - batch * spare, 0), spare)
-        if taken:
-            pieces.append(probes_ref[batch * spare:batch * spare + taken, :])
-        if taken < spare:
-            pieces.append(jnp.zeros((spare - taken, columns), jnp.float32))
     high, low = split(modes_ref[...])
-    field_high, field_low = split(jnp.concatenate(pieces, axis=0))
-    all_high = jnp.concatenate([high, field_high], axis=0)
-    all_low = jnp.concatenate([low, field_low], axis=0)
-    modes_out[...] += nt_pass(high, all_high) + (nt_pass(high, all_low) + nt_pass(low, all_high))
-    snap_high, snap_low = split(snaps_ref[...].reshape(count * width, columns))
-    snaps_out[...] += nt_pass(snap_high, field_high) + (
-        nt_pass(snap_high, field_low) + nt_pass(snap_low, field_high)
+    snap_high, snap_low = split(snaps_ref[...].reshape(snap_count, columns))
+    probe_high, probe_low = split(probes_ref[...])
+    norms_out[...] += nt_pass(high, high)
+    cross_out[...] += nt_pass(low, high)
+    past_snaps[...] += nt_pass(snap_high, high) + (nt_pass(snap_low, high) + nt_pass(snap_high, low))
+    past_probes[...] += nt_pass(probe_high, high) + (nt_pass(probe_low, high) + nt_pass(probe_high, low))
+    own_out[...] += nt_pass(snap_high, snap_high)
+    own_cross[...] += nt_pass(snap_low, snap_high)
+    others_out[...] += nt_pass(snap_high, probe_high) + (
+        nt_pass(snap_low, probe_high) + nt_pass(snap_high, probe_low)
     )
 
     @pl.when(step == pl.num_programs(0) - 1)
     def _():
-        rank = modes_ref.shape[0]
         half = rank // 2
-        blocks = [
-            modes_out[:half, :half],
-            modes_out[half:, :half],
-            modes_out[half:, half:rank],
-        ]
+        spare = LANES - width
+        cross = cross_out[...]
+        norms = norms_out[...] + (cross + cross.T)
+        blocks = [norms[:half, :half], norms[half:, :half], norms[half:, half:]]
         for batch in range(count):
-            tile = slice(rank + batch * LANES, rank + (batch + 1) * LANES)
-            block = modes_out[:, tile]
+            tile = [past_snaps[batch * width:(batch + 1) * width, :]]
+            taken = min(max(probe_count - batch * spare, 0), spare)
+            if taken:
+                tile.append(past_probes[batch * spare:batch * spare + taken, :])
+            if taken < spare:
+                tile.append(jnp.zeros((spare - taken, rank), jnp.float32))
+            tile = jnp.concatenate(tile, axis=0)
+            block = jnp.concatenate([tile[:, :half].T, tile[:, half:].T], axis=0)
             blocks.append(block if batch + 1 < count else fold(block))
+        cross = jnp.concatenate(
+            [own_cross[...], jnp.zeros((snap_count, rank - snap_count), jnp.float32)], axis=1
+        )
+        cross = jnp.concatenate([cross, jnp.zeros((rank - snap_count, rank), jnp.float32)], axis=0)
+        own = own_out[...] + (own_cross[...] + cross.T[:snap_count, :snap_count])
         for batch in range(count):
-            block = snaps_out[:, batch * LANES:(batch + 1) * LANES]
+            tile = [own[:, batch * width:(batch + 1) * width]]
+            taken = min(max(probe_count - batch * spare, 0), spare)
+            if taken:
+                tile.append(others_out[:, batch * spare:batch * spare + taken])
+            if taken < spare:
+                tile.append(jnp.zeros((snap_count, spare - taken), jnp.float32))
+            block = jnp.concatenate(tile, axis=1)
             blocks.append(block if batch + 1 < count else fold(block))
         at = 0
         for block in blocks:
             packed_ref[at:at + block.shape[0], :] = block * scale
             at += block.shape[0]
+        if at < packed_ref.shape[0]:
+            packed_ref[at:, :] = jnp.zeros((packed_ref.shape[0] - at, LANES), jnp.float32)
 
 
 def local_grams(modes, snaps, probes, scale):
     rank, columns = modes.shape
     count, width, _ = snaps.shape
     probe_count = probes.shape[0]
-    fields = count * LANES
     tile = 1024
     rows = packed_rows(rank, count * width, count)
     return pl.pallas_call(
@@ -233,34 +248,47 @@
         out_specs=pl.BlockSpec((rows, LANES), lambda i: (0, 0)),
         out_shape=jax.ShapeDtypeStruct((rows, LANES), jnp.float32),
         scratch_shapes=[
-            pltpu.VMEM((rank, rank + fields), jnp.float32),
-            pltpu.VMEM((count * width, fields), jnp.float32),
+            pltpu.VMEM(shape, jnp.float32)
+            for shape in (
+                (rank, rank), (rank, rank), (count * width, rank), (probe_count, rank),
+                (count * width, count * width), (count * width, count * width), (count * width, probe_count),
+            )
         ],
-        compiler_params=pltpu.CompilerParams(vmem_limit_bytes=48 << 20),
+        compiler_params=pltpu.CompilerParams(vmem_limit_bytes=60 << 20),
         name="grams",
     )(modes, snaps, probes)
 
 
 def sum_over_devices(part, size):
-    def swap(value, bit):
-        return lax.ppermute(value, AXES, [(i, i ^ bit) for i in range(size)])
+    def swap(value, mask):
+        return lax.ppermute(value, AXES, [(i, i ^ mask) for i in range(size)])
 
     bits = size.bit_length() - 1
-    if size != 1 << bits or bits < 2:
+    if size != 1 << bits or bits < 3 or part.shape[0] % (8 * GROUP):
         return lax.psum(part, AXES)
-    odd = lax.rem(lax.axis_index(AXES), 2) == 1
+    index = lax.axis_index(AXES)
+    odd = lax.rem(index, 2) == 1
     half = part.shape[0] // 2
     low, high = part[:half], part[half:]
     part = jnp.where(odd, high, low) + swap(jnp.where(odd, low, high), 1)
-    order = list(range(1, bits))
-    chunk = -(-half // (3 * GROUP)) * GROUP
-    chunks = [part[at:at + chunk] for at in range(0, half, chunk)]
-    for turn in range(bits - 1):
-        chunks = [
-            piece + swap(piece, 1 << order[(turn + number) % len(order)])
-            for number, piece in enumerate(chunks)
-        ]
-    part = jnp.concatenate(chunks, axis=0)
+    place = lax.rem(lax.div(index, 2), 4)
+    rows = half // 4
+
+    def quarter(mask):
+        return lax.dynamic_slice_in_dim(part, jnp.bitwise_xor(place, mask) * rows, rows, 0)
+
+    received = [swap(quarter(mask), 2 * mask) for mask in (1, 2, 3)]
+    total = quarter(0) + received[0] + received[1] + received[2]
+    for bit in range(3, bits):
+        total = total + swap(total, 1 << bit)
+    gathered = jnp.stack([total] + [swap(total, 2 * mask) for mask in (1, 2, 3)], axis=0)
+    part = jnp.concatenate(
+        [
+            lax.dynamic_index_in_dim(gathered, jnp.bitwise_xor(place, at), 0, keepdims=False)
+            for at in range(4)
+        ],
+        axis=0,
+    )
     other = swap(part, 1)
     return jnp.concatenate([jnp.where(odd, other, part), jnp.where(odd, part, other)], axis=0)
 
@@ -280,12 +308,37 @@
 
 
 def core_kernel(
-    packed_ref, core_ref, mix_ref, energy_out, captured_ref, energy_ref, norms_ref, inner_ref, snaps_ref, kept_ref
+    packed_ref,
+    core_ref,
+    modes_hbm,
+    snaps_hbm,
+    new_hbm,
+    core_out,
+    captured_ref,
+    energy_ref,
+    norms_ref,
+    inner_ref,
+    snaps_ref,
+    kept_ref,
+    rows_ref,
+    new_ref,
+    in_sems,
+    out_sems,
 ):
+    loads = [pltpu.make_async_copy(modes_hbm, rows_ref.at[pl.ds(0, modes_hbm.shape[0])], in_sems.at[0])]
+    for batch in range(snaps_hbm.shape[0]):
+        at = modes_hbm.shape[0] + batch * snaps_hbm.shape[1]
+        loads.append(
+            pltpu.make_async_copy(
+                snaps_hbm.at[batch], rows_ref.at[pl.ds(at, snaps_hbm.shape[1])], in_sems.at[1 + batch]
+            )
+        )
+    for load in loads:
+        load.start()
     rank = core_ref.shape[0]
     batches = captured_ref.shape[0]
     width = snaps_ref.shape[0] // batches
-    probes = captured_ref.shape[2] - batches * width
+    probes = captured_ref.shape[1] - batches * width
     half = rank // 2
     norms_ref[:half, :half] = packed_ref[:half, :]
     norms_ref[half:, :half] = packed_ref[half:rank, :]
@@ -350,120 +403,91 @@
         )
         kept_ref[...] = product(old, split(kept_ref[...]), False)
         kept_ref[:, pl.ds(pl.multiple_of(rank + batch * LANES, LANES), LANES)] = low
-        captured_ref[batch] = jnp.concatenate(
-            [inner_ref[:, b * LANES:b * LANES + width] for b in range(batches)]
-            + [
-                inner_ref[:, b * LANES + width:(b + 1) * LANES]
-                for b in range(probes // (LANES - width))
-            ],
-            axis=1,
-        )
+        for number in range(batches):
+            tile = inner_ref[:, number * LANES:(number + 1) * LANES]
+            turned = jnp.concatenate([tile[at:at + LANES, :].T for at in range(0, rank, LANES)], axis=1)
+            captured_ref[batch, number * width:(number + 1) * width, :] = turned[:width, :]
+            room = LANES - width
+            taken = min(max(probes - number * room, 0), room)
+            if taken:
+                at = batches * width + number * room
+                captured_ref[batch, at:at + taken, :] = turned[width:width + taken, :]
         return carry
 
     lax.fori_loop(0, batches, absorb, 0)
-    mix_ref[...] = jnp.concatenate(
+    mix = jnp.concatenate(
         [kept_ref[:, :rank]]
         + [kept_ref[:, rank + b * LANES:rank + b * LANES + width] for b in range(batches)],
         axis=1,
     )
-    energy_out[...] = energy_ref[...]
-
-
-def small_algebra(packed, core, batches, width, probes):
-    rank = core.shape[0]
+    mix_high, mix_low = split(mix)
+
+    def one(left, right):
+        return lax.dot_general(
+            left, right, (((1,), (0,)), ((), ())), preferred_element_type=jnp.float32
+        )
+
+    for load in loads:
+        load.wait()
+    blocks = rank // PANEL
+    columns = rows_ref.shape[1] // blocks
+    piece = columns // (PANEL // GROUP)
+    stores = []
+    for number in range(blocks):
+        start = number * PANEL
+        end = start + PANEL
+        steps = eliminate_panel(energy_ref[start:end, :], start, False)
+        for part in range(PANEL // GROUP):
+            at = number * columns + part * piece
+            high, low = split(rows_ref[:, at:at + piece])
+            new_ref[:, at:at + piece] = one(mix_high, high) + (one(mix_high, low) + one(mix_low, high))
+            next(steps)
+        block = pl.ds(number * columns, columns)
+        stores.append(
+            pltpu.make_async_copy(new_ref.at[:, block], new_hbm.at[:, block], out_sems.at[number])
+        )
+        stores[-1].start()
+        panel = finish(steps)
+        energy_ref[start:end, :] = panel
+        if end < rank:
+            energy_ref[end:, :] = energy_ref[end:, :] - stacked_square(panel, end)
+    lane = lax.broadcasted_iota(jnp.int32, (rank, rank), 1)
+    row = lax.broadcasted_iota(jnp.int32, (rank, rank), 0)
+    core_out[...] = jnp.where(lane >= row, energy_ref[...], 0.0).T
+    for store in stores:
+        store.wait()
+
+
+def updated(packed, core, modes, snaps, probes):
+    rank, columns = modes.shape
+    batches, width, _ = snaps.shape
     snap_count = batches * width
-    columns = batches * LANES
+    tiles = batches * LANES
+    whole = pl.BlockSpec(memory_space=pltpu.VMEM)
+    apart = pl.BlockSpec(memory_space=pl.ANY)
     return pl.pallas_call(
         core_kernel,
+        in_specs=[whole, whole, apart, apart],
+        out_specs=[apart, whole, whole],
         out_shape=[
-            jax.ShapeDtypeStruct((rank, rank + snap_count), jnp.float32),
+            jax.ShapeDtypeStruct((rank, columns), jnp.float32),
             jax.ShapeDtypeStruct((rank, rank), jnp.float32),
-            jax.ShapeDtypeStruct((batches, rank, snap_count + probes), jnp.float32),
+            jax.ShapeDtypeStruct((batches, snap_count + probes, rank), jnp.float32),
         ],
         scratch_shapes=[
             pltpu.VMEM((rank, rank), jnp.float32),
             pltpu.VMEM((rank, rank), jnp.float32),
+            pltpu.VMEM((rank, tiles), jnp.float32),
+            pltpu.VMEM((snap_count, tiles), jnp.float32),
+            pltpu.VMEM((rank, rank + tiles), jnp.float32),
+            pltpu.VMEM((rank + snap_count, columns), jnp.float32),
             pltpu.VMEM((rank, columns), jnp.float32),
-            pltpu.VMEM((snap_count, columns), jnp.float32),
-            pltpu.VMEM((rank, rank + columns), jnp.float32),
+            pltpu.SemaphoreType.DMA((1 + batches,)),
+            pltpu.SemaphoreType.DMA((rank // PANEL,)),
         ],
-        compiler_params=pltpu.CompilerParams(vmem_limit_bytes=48 << 20),
+        compiler_params=pltpu.CompilerParams(vmem_limit_bytes=52 << 20),
         name="core_updates",
-    )(packed, core)
-
-
-def apply_kernel(mix_ref, energy_ref, modes_ref, snaps_ref, out_ref, core_ref, mixed_ref, left_ref):
-    step = pl.program_id(0)
-    count, width, columns = snaps_ref.shape
-    rank = energy_ref.shape[0]
-
-    @pl.when(step == 0)
-    def _():
-        left_ref[...] = energy_ref[...]
-        high, low = split(mix_ref[...])
-        mixed_ref[0] = high
-        mixed_ref[1] = low
-
-    def one(left, right):
-        return lax.dot_general(
-            left, right, (((1,), (0,)), ((), ())), preferred_element_type=jnp.float32
-        )
-
-    def block_of(start):
-        end = start + FINAL_PANEL
-        steps = eliminate_panel(left_ref[start:end, :], start, False)
-        piece = columns // (FINAL_PANEL // GROUP)
-        for number in range(FINAL_PANEL // GROUP):
-            part = slice(number * piece, (number + 1) * piece)
-            rows = jnp.concatenate(
-                [modes_ref[:, part], snaps_ref[:, :, part].reshape(count * width, piece)], axis=0
-            )
-            high, low = split(rows)
-            mix_high, mix_low = mixed_ref[0], mixed_ref[1]
-            out_ref[:, part] = one(mix_high, high) + (one(mix_high, low) + one(mix_low, high))
-            next(steps)
-        panel = finish(steps)
-        left_ref[start:end, :] = panel
-        if end < rank:
-            left_ref[end:, :] = left_ref[end:, :] - tn(panel[:, end:], panel)
-        else:
-            lane = lax.broadcasted_iota(jnp.int32, (rank, rank), 1)
-            row = lax.broadcasted_iota(jnp.int32, (rank, rank), 0)
-            core_ref[...] = jnp.where(lane >= row, left_ref[...], 0.0).T
-
-    for number in range(rank // FINAL_PANEL):
-        pl.when(step == number)(functools.partial(block_of, number * FINAL_PANEL))
-
-
-def apply_mix(mix, energy, modes, snaps):
-    rank, columns = modes.shape
-    count, width, _ = snaps.shape
-    steps = rank // FINAL_PANEL
-    tile = columns // steps
-    return pl.pallas_call(
-        apply_kernel,
-        grid=(steps,),
-        in_specs=[
-            pl.BlockSpec(mix.shape, lambda i: (0, 0)),
-            pl.BlockSpec(energy.shape, lambda i: (0, 0)),
-            pl.BlockSpec((rank, tile), lambda i: (0, i)),
-            pl.BlockSpec((count, width, tile), lambda i: (0, 0, i)),
-        ],
-        out_specs=[
-            pl.BlockSpec((rank, tile), lambda i: (0, i)),
-            pl.BlockSpec((rank, rank), lambda i: (0, 0)),
-        ],
-        out_shape=[
-            jax.ShapeDtypeStruct((rank, columns), jnp.float32),
-            jax.ShapeDtypeStruct((rank, rank), jnp.float32),
-        ],
-        scratch_shapes=[
-            pltpu.VMEM((2,) + mix.shape, jnp.bfloat16),
-            pltpu.VMEM((rank, rank), jnp.float32),
-        ],
-        compiler_params=pltpu.CompilerParams(vmem_limit_bytes=48 << 20),
-        name="new_basis",
-    )(mix, energy, modes, snaps)
+    )(packed, core, modes, snaps)
 
 
 def body(modes, snaps, probes, core, *, devices):
@@ -471,9 +495,8 @@
     batches, width, _ = snaps.shape
     scale = 1.0 / (columns * devices)
     packed = sum_over_devices(local_grams(modes, snaps, probes, scale), devices)
-    mix, energy, captured = small_algebra(packed, core, batches, width, probes.shape[0])
-    new_modes, new_core = apply_mix(mix, energy, modes, snaps)
-    return new_modes, new_core, captured
+    new_modes, new_core, captured = updated(packed, core, modes, snaps, probes.shape[0])
+    return new_modes, new_core, jnp.swapaxes(captured, 1, 2)
 
 
 def solution(mesh):

time: 134 us -> 121 us (0.903)
  Pallas kernels: 90.1 us -> 85.1 us
  waiting for transfers between devices: 23 us -> 19.3 us
  starting transfers between devices: 16.4 us -> 12.9 us
  local copies, waits for them, and re-layouts: 3.51 us -> 0.07 us
  other arithmetic: 0.48 us -> 2.58 us
    pallas_call x2 -> x1, Pallas kernels: 70.7 us -> 66.4 us  [updated(): pl.pallas_call(core_kernel, in_specs=[whole, whole, apart, apart], out_sp...]
    ppermute x14 -> x10, waiting for transfers between devices: 23 us -> 19.3 us  [swap(): return lax.ppermute(value, AXES, [(i, i ^ mask) for i in range(size)])]
    unnamed x5 -> x2, local copies, waits for them, and re-layouts: 3.49 us -> 0.01 us
    ppermute x14 -> x10, starting transfers between devices: 16.4 us -> 12.9 us  [swap(): return lax.ppermute(value, AXES, [(i, i ^ mask) for i in range(size)])]
  transfers between devices with their start and end apart: 14 -> 10, of which waited for: 8 -> 10; matrix products, arithmetic and copies ran while one was open for 0% -> 0% of each run, Pallas kernels for 0% -> 0%
where the time goes in v3:
time: 121 us
  Pallas kernels  85.1 us (70%)
  waiting for transfers between devices  19.3 us (16%)
  starting transfers between devices  12.9 us (11%)
  other arithmetic  2.58 us (2%)
    pallas_call x1, Pallas kernels, updated(): pl.pallas_call(core_kernel, in_specs=[whole, whole, apart, apart], out_sp...  66.4 us
    ppermute x10, waiting for transfers between devices, swap(): return lax.ppermute(value, AXES, [(i, i ^ mask) for i in range(size)])  19.3 us
    pallas_call x1, Pallas kernels, local_grams(): pl.pallas_call(functools.partial(gram_kernel, scale), grid=(columns // ti...  18.7 us
    ppermute x10, starting transfers between devices, swap(): return lax.ppermute(value, AXES, [(i, i ^ mask) for i in range(size)])  12.9 us
  transfers between devices with their start and end apart: 10, of which 10 were waited for; matrix products, arithmetic and copies ran while one was open for 0% of the time, Pallas kernels for 0%

profile of v3, /device:TPU:0, one launch (start us, length us, event | category | flops | bytes accessed | tf_op | source)
XLA Modules:
  0.0 120.9 jit_solution(14861245282633182019)
XLA Ops:
  0.6 18.7 %grams.1 = f32[1536,128]{1,0:T(8,128)} custom-call(f32[256,8192]{1,0:T(8,128)} %modes_hbm.1, f32[3,64,8192]{2,1,0:T(8,128)} %snaps_hbm.1, f32[128,8192]{1,0:T(8,128)} %probes_ref.1), custom_call_target="tpu_custom_call" | custom-call | tf_op jit(solution)/shard_map/grams/pallas_call | solution.py:240
  19.3 0.0 copy-start
  19.3 1.2 slice_select_fusion
  20.5 0.5 collective-permute-start
  21.1 1.3 %collective-permute-done = f32[768,128]{1,0:T(8,128)S(1)} collective-permute-done((f32[768,128]{1,0:T(8,128)S(1)}, f32[768,128]{1,0:T(8,128)S(1)}, u32[]{:S(2)}, u32[]{:S(2)}) %collective-permute-start) | collective-permute-done | bytes 393248 | tf_op jit(solution)/shard_map/ppermute | solution.py:264
  22.4 1.2 select_add_fusion
  23.6 2.9 %collective-permute-start.1 = (f32[192,128]{1,0:T(8,128)S(1)}, f32[192,128]{1,0:T(8,128)S(1)}, u32[]{:S(2)}, u32[]{:S(2)}) collective-permute-start(f32[192,128]{1,0:T(8,128)S(1)} %get-tuple-element.15), channel_id=1, source_target_pairs={{0,2},{1,3},{2,0},{3,1},{4,6},{5,7},{6,4},{7,5},{8,10},{9,11},{10,... | collective-permute-start | bytes 294920 | tf_op jit(solution)/shard_map/ppermute | solution.py:264
  26.6 1.5 %collective-permute-start.3 = (f32[192,128]{1,0:T(8,128)S(1)}, f32[192,128]{1,0:T(8,128)S(1)}, u32[]{:S(2)}, u32[]{:S(2)}) collective-permute-start(f32[192,128]{1,0:T(8,128)S(1)} %get-tuple-element.16), channel_id=1, source_target_pairs={{0,6},{1,7},{2,4},{3,5},{4,2},{5,3},{6,0},{7,1},{8,14},{9,15},{10,... | collective-permute-start | bytes 294920 | tf_op jit(solution)/shard_map/ppermute | solution.py:264
  28.0 0.1 collective-permute-start.2
  28.1 1.6 %collective-permute-done.1 = f32[192,128]{1,0:T(8,128)S(1)} collective-permute-done((f32[192,128]{1,0:T(8,128)S(1)}, f32[192,128]{1,0:T(8,128)S(1)}, u32[]{:S(2)}, u32[]{:S(2)}) %collective-permute-start.1) | collective-permute-done | bytes 98336 | tf_op jit(solution)/shard_map/ppermute | solution.py:264
  29.7 3.3 %collective-permute-done.3 = f32[192,128]{1,0:T(8,128)S(1)} collective-permute-done((f32[192,128]{1,0:T(8,128)S(1)}, f32[192,128]{1,0:T(8,128)S(1)}, u32[]{:S(2)}, u32[]{:S(2)}) %collective-permute-start.3) | collective-permute-done | bytes 98336 | tf_op jit(solution)/shard_map/ppermute | solution.py:264
  33.1 1.3 %collective-permute-done.2 = f32[192,128]{1,0:T(8,128)S(1)} collective-permute-done((f32[192,128]{1,0:T(8,128)S(1)}, f32[192,128]{1,0:T(8,128)S(1)}, u32[]{:S(2)}, u32[]{:S(2)}) %collective-permute-start.2) | collective-permute-done | bytes 98336 | tf_op jit(solution)/shard_map/ppermute | solution.py:264
  34.4 1.6 %collective-permute-start.4 = (f32[192,128]{1,0:T(8,128)S(1)}, f32[192,128]{1,0:T(8,128)S(1)}, u32[]{:S(2)}, u32[]{:S(2)}) collective-permute-start(f32[192,128]{1,0:T(8,128)S(1)} %add_add_fusion), channel_id=1, source_target_pairs={{0,8},{1,9},{2,10},{3,11},{4,12},{5,13},{6,14},{7,15},{8,0},{9,1},... | collective-permute-start | bytes 294920 | tf_op jit(solution)/shard_map/ppermute | solution.py:264
  36.0 3.0 %collective-permute-done.4 = f32[192,128]{1,0:T(8,128)S(1)} collective-permute-done((f32[192,128]{1,0:T(8,128)S(1)}, f32[192,128]{1,0:T(8,128)S(1)}, u32[]{:S(2)}, u32[]{:S(2)}) %collective-permute-start.4) | collective-permute-done | bytes 98336 | tf_op jit(solution)/shard_map/ppermute | solution.py:264
  39.1 2.7 %collective-permute-start.5 = (f32[192,128]{1,0:T(8,128)S(1)}, f32[192,128]{1,0:T(8,128)S(1)}, u32[]{:S(2)}, u32[]{:S(2)}) collective-permute-start(f32[192,128]{1,0:T(8,128)S(1)} %add.55), channel_id=1, source_target_pairs={{0,16},{1,17},{2,18},{3,19},{4,20},{5,21},{6,22},{7,23},{8,24},{9,... | collective-permute-start | bytes 294920 | tf_op jit(solution)/shard_map/ppermute | solution.py:264
  41.7 2.9 %collective-permute-done.5 = f32[192,128]{1,0:T(8,128)S(1)} collective-permute-done((f32[192,128]{1,0:T(8,128)S(1)}, f32[192,128]{1,0:T(8,128)S(1)}, u32[]{:S(2)}, u32[]{:S(2)}) %collective-permute-start.5) | collective-permute-done | bytes 98336 | tf_op jit(solution)/shard_map/ppermute | solution.py:264
  44.7 1.5 %collective-permute-start.8 = (f32[192,128]{1,0:T(8,128)S(1)}, f32[192,128]{1,0:T(8,128)S(1)}, u32[]{:S(2)}, u32[]{:S(2)}) collective-permute-start(f32[192,128]{1,0:T(8,128)S(1)} %add.56), channel_id=1, source_target_pairs={{0,6},{1,7},{2,4},{3,5},{4,2},{5,3},{6,0},{7,1},{8,14},{9,15},{10,... | collective-permute-start | bytes 294920 | tf_op jit(solution)/shard_map/ppermute | solution.py:264
  46.2 1.5 %collective-permute-start.7 = (f32[192,128]{1,0:T(8,128)S(1)}, f32[192,128]{1,0:T(8,128)S(1)}, u32[]{:S(2)}, u32[]{:S(2)}) collective-permute-start(f32[192,128]{1,0:T(8,128)S(1)} %add.56), channel_id=1, source_target_pairs={{0,4},{1,5},{2,6},{3,7},{4,0},{5,1},{6,2},{7,3},{8,12},{9,13},{10,... | collective-permute-start | bytes 294920 | tf_op jit(solution)/shard_map/ppermute | solution.py:264
  47.7 0.5 collective-permute-start.6
  48.2 2.1 %collective-permute-done.8 = f32[192,128]{1,0:T(8,128)S(1)} collective-permute-done((f32[192,128]{1,0:T(8,128)S(1)}, f32[192,128]{1,0:T(8,128)S(1)}, u32[]{:S(2)}, u32[]{:S(2)}) %collective-permute-start.8) | collective-permute-done | bytes 98336 | tf_op jit(solution)/shard_map/ppermute | solution.py:264
  50.3 1.0 collective-permute-done.7
  51.3 1.0 collective-permute-done.6
  52.4 0.1 collective-permute-start.9
  52.5 1.7 %collective-permute-done.9 = f32[768,128]{1,0:T(8,128)S(1)} collective-permute-done((f32[768,128]{1,0:T(8,128)S(1)}, f32[768,128]{1,0:T(8,128)S(1)}, u32[]{:S(2)}, u32[]{:S(2)}) %collective-permute-start.9) | collective-permute-done | bytes 393248 | tf_op jit(solution)/shard_map/ppermute | solution.py:264
  54.2 0.1 broadcast_select_fusion.1
  54.3 0.1 pad_maximum_fusion.packed_ref
  54.3 0.0 copy-done
  54.3 66.4 %core_updates.1 = (f32[256,8192]{1,0:T(8,128)}, f32[256,256]{1,0:T(8,128)}, f32[3,320,256]{2,1,0:T(8,128)}) custom-call(f32[1536,128]{1,0:T(8,128)S(1)} %pad_maximum_fusion.packed_ref, f32[256,256]{1,0:T(8,128)S(1)} %copy-done, f32[256,8192]{1,0:T(8,128)} %modes_hbm.1, f32[3,64,8192]{2,1,0:T(8,128)} %snaps_hbm.1), custom_call_target="tpu_custom_call" | custom-call | tf_op jit(solution)/shard_map/core_updates/pallas_call | solution.py:468
  (7 shorter events, 0.2 us)
Async XLA Ops:
  19.3 35.0 %copy-start = (f32[256,256]{1,0:T(8,128)S(1)}, f32[256,256]{1,0:T(8,128)}, u32[]{:S(2)}) copy-start(f32[256,256]{1,0:T(8,128)} %core_ref.1) | copy-start | bytes 786436
  20.5 1.9 %collective-permute-start = (f32[768,128]{1,0:T(8,128)S(1)}, f32[768,128]{1,0:T(8,128)S(1)}, u32[]{:S(2)}, u32[]{:S(2)}) collective-permute-start(f32[768,128]{1,0:T(8,128)S(1)} %slice_select_fusion), channel_id=1, source_target_pairs={{0,1},{1,0},{2,3},{3,2},{4,5},{5,4},{6,7},{7,6},{8,9},{9,8},{10,11... | collective-permute-start | bytes 1179656 | tf_op jit(solution)/shard_map/ppermute | solution.py:264
  23.6 6.1 %collective-permute-start.1 = (f32[192,128]{1,0:T(8,128)S(1)}, f32[192,128]{1,0:T(8,128)S(1)}, u32[]{:S(2)}, u32[]{:S(2)}) collective-permute-start(f32[192,128]{1,0:T(8,128)S(1)} %get-tuple-element.15), channel_id=1, source_target_pairs={{0,2},{1,3},{2,0},{3,1},{4,6},{5,7},{6,4},{7,5},{8,10},{9,11},{10,... | collective-permute-start | bytes 294920 | tf_op jit(solution)/shard_map/ppermute | solution.py:264
  26.6 6.5 %collective-permute-start.3 = (f32[192,128]{1,0:T(8,128)S(1)}, f32[192,128]{1,0:T(8,128)S(1)}, u32[]{:S(2)}, u32[]{:S(2)}) collective-permute-start(f32[192,128]{1,0:T(8,128)S(1)} %get-tuple-element.16), channel_id=1, source_target_pairs={{0,6},{1,7},{2,4},{3,5},{4,2},{5,3},{6,0},{7,1},{8,14},{9,15},{10,... | collective-permute-start | bytes 294920 | tf_op jit(solution)/shard_map/ppermute | solution.py:264
  28.0 6.3 %collective-permute-start.2 = (f32[192,128]{1,0:T(8,128)S(1)}, f32[192,128]{1,0:T(8,128)S(1)}, u32[]{:S(2)}, u32[]{:S(2)}) collective-permute-start(f32[192,128]{1,0:T(8,128)S(1)} %get-tuple-element.17), channel_id=1, source_target_pairs={{0,4},{1,5},{2,6},{3,7},{4,0},{5,1},{6,2},{7,3},{8,12},{9,13},{10,... | collective-permute-start | bytes 294920 | tf_op jit(solution)/shard_map/ppermute | solution.py:264
  34.4 4.7 %collective-permute-start.4 = (f32[192,128]{1,0:T(8,128)S(1)}, f32[192,128]{1,0:T(8,128)S(1)}, u32[]{:S(2)}, u32[]{:S(2)}) collective-permute-start(f32[192,128]{1,0:T(8,128)S(1)} %add_add_fusion), channel_id=1, source_target_pairs={{0,8},{1,9},{2,10},{3,11},{4,12},{5,13},{6,14},{7,15},{8,0},{9,1},... | collective-permute-start | bytes 294920 | tf_op jit(solution)/shard_map/ppermute | solution.py:264
  39.1 5.6 %collective-permute-start.5 = (f32[192,128]{1,0:T(8,128)S(1)}, f32[192,128]{1,0:T(8,128)S(1)}, u32[]{:S(2)}, u32[]{:S(2)}) collective-permute-start(f32[192,128]{1,0:T(8,128)S(1)} %add.55), channel_id=1, source_target_pairs={{0,16},{1,17},{2,18},{3,19},{4,20},{5,21},{6,22},{7,23},{8,24},{9,... | collective-permute-start | bytes 294920 | tf_op jit(solution)/shard_map/ppermute | solution.py:264
  44.7 5.6 %collective-permute-start.8 = (f32[192,128]{1,0:T(8,128)S(1)}, f32[192,128]{1,0:T(8,128)S(1)}, u32[]{:S(2)}, u32[]{:S(2)}) collective-permute-start(f32[192,128]{1,0:T(8,128)S(1)} %add.56), channel_id=1, source_target_pairs={{0,6},{1,7},{2,4},{3,5},{4,2},{5,3},{6,0},{7,1},{8,14},{9,15},{10,... | collective-permute-start | bytes 294920 | tf_op jit(solution)/shard_map/ppermute | solution.py:264
  46.2 5.1 %collective-permute-start.7 = (f32[192,128]{1,0:T(8,128)S(1)}, f32[192,128]{1,0:T(8,128)S(1)}, u32[]{:S(2)}, u32[]{:S(2)}) collective-permute-start(f32[192,128]{1,0:T(8,128)S(1)} %add.56), channel_id=1, source_target_pairs={{0,4},{1,5},{2,6},{3,7},{4,0},{5,1},{6,2},{7,3},{8,12},{9,13},{10,... | collective-permute-start | bytes 294920 | tf_op jit(solution)/shard_map/ppermute | solution.py:264
  47.7 4.6 %collective-permute-start.6 = (f32[192,128]{1,0:T(8,128)S(1)}, f32[192,128]{1,0:T(8,128)S(1)}, u32[]{:S(2)}, u32[]{:S(2)}) collective-permute-start(f32[192,128]{1,0:T(8,128)S(1)} %add.56), channel_id=1, source_target_pairs={{0,2},{1,3},{2,0},{3,1},{4,6},{5,7},{6,4},{7,5},{8,10},{9,11},{10,... | collective-permute-start | bytes 294920 | tf_op jit(solution)/shard_map/ppermute | solution.py:264
  52.4 1.8 %collective-permute-start.9 = (f32[768,128]{1,0:T(8,128)S(1)}, f32[768,128]{1,0:T(8,128)S(1)}, u32[]{:S(2)}, u32[]{:S(2)}) collective-permute-start(f32[768,128]{1,0:T(8,128)S(1)} %pad_maximum_fusion.2), channel_id=1, source_target_pairs={{0,1},{1,0},{2,3},{3,2},{4,5},{5,4},{6,7},{7,6},{8,9},{9,8},{10,11... | collective-permute-start | bytes 1179656 | tf_op jit(solution)/shard_map/ppermute | solution.py:264

commit v4 on v3

--- a/solution.py
+++ b/solution.py
@@ -188,8 +188,8 @@
     past_probes[...] += nt_pass(probe_high, high) + (nt_pass(probe_low, high) + nt_pass(probe_high, low))
     own_out[...] += nt_pass(snap_high, snap_high)
     own_cross[...] += nt_pass(snap_low, snap_high)
-    others_out[...] += nt_pass(snap_high, probe_high) + (
-        nt_pass(snap_low, probe_high) + nt_pass(snap_high, probe_low)
+    others_out[...] += nt_pass(probe_high, snap_high) + (
+        nt_pass(probe_low, snap_high) + nt_pass(probe_high, snap_low)
     )
 
     @pl.when(step == pl.num_programs(0) - 1)
@@ -213,12 +213,16 @@
             [own_cross[...], jnp.zeros((snap_count, rank - snap_count), jnp.float32)], axis=1
         )
         cross = jnp.concatenate([cross, jnp.zeros((rank - snap_count, rank), jnp.float32)], axis=0)
+        others = jnp.concatenate(
+            [others_out[...], jnp.zeros((probe_count, rank - snap_count), jnp.float32)], axis=1
+        )
+        others = jnp.concatenate([others[:, :half].T, others[:, half:].T], axis=0)[:snap_count, :]
         own = own_out[...] + (own_cross[...] + cross.T[:snap_count, :snap_count])
         for batch in range(count):
             tile = [own[:, batch * width:(batch + 1) * width]]
             taken = min(max(probe_count - batch * spare, 0), spare)
             if taken:
-                tile.append(others_out[:, batch * spare:batch * spare + taken])
+                tile.append(others[:, batch * spare:batch * spare + taken])
             if taken < spare:
                 tile.append(jnp.zeros((snap_count, spare - taken), jnp.float32))
             block = jnp.concatenate(tile, axis=1)
@@ -251,7 +255,7 @@
             pltpu.VMEM(shape, jnp.float32)
             for shape in (
                 (rank, rank), (rank, rank), (count * width, rank), (probe_count, rank),
-                (count * width, count * width), (count * width, count * width), (count * width, probe_count),
+                (count * width, count * width), (count * width, count * width), (probe_count, count * width),
             )
         ],
         compiler_params=pltpu.CompilerParams(vmem_limit_bytes=60 << 20),
@@ -267,10 +271,11 @@
     if size != 1 << bits or bits < 3 or part.shape[0] % (8 * GROUP):
         return lax.psum(part, AXES)
     index = lax.axis_index(AXES)
-    odd = lax.rem(index, 2) == 1
+    core = lax.rem(index, 2)
+    odd = core == 1
     half = part.shape[0] // 2
-    low, high = part[:half], part[half:]
-    part = jnp.where(odd, high, low) + swap(jnp.where(odd, low, high), 1)
+    away = swap(lax.dynamic_slice_in_dim(part, (1 - core) * half, half, 0), 1)
+    part = lax.dynamic_slice_in_dim(part, core * half, half, 0) + away
     place = lax.rem(lax.div(index, 2), 4)
     rows = half // 4
 

time: 121 us -> 120 us (level)
  other arithmetic: 2.58 us -> 1.24 us
where the time goes in v4:
time: 120 us
  Pallas kernels  84.5 us (70%)
  waiting for transfers between devices  19.4 us (16%)
  starting transfers between devices  12.9 us (11%)
  other arithmetic  1.24 us (1%)
    pallas_call x1, Pallas kernels, updated(): pl.pallas_call(core_kernel, in_specs=[whole, whole, apart, apart], out_sp...  66.4 us
    ppermute x10, waiting for transfers between devices, swap(): return lax.ppermute(value, AXES, [(i, i ^ mask) for i in range(size)])  19.4 us
    pallas_call x1, Pallas kernels, local_grams(): pl.pallas_call(functools.partial(gram_kernel, scale), grid=(columns // ti...  18.1 us
    ppermute x10, starting transfers between devices, swap(): return lax.ppermute(value, AXES, [(i, i ^ mask) for i in range(size)])  12.9 us
  transfers between devices with their start and end apart: 10, of which 10 were waited for; matrix products, arithmetic and copies ran while one was open for 0% of the time, Pallas kernels for 0%

profile of v4, /device:TPU:0, one launch (start us, length us, event | category | flops | bytes accessed | tf_op | source)
XLA Modules:
  0.0 120.0 jit_solution(5317282060903179524)
XLA Ops:
  0.6 18.1 %grams.1 = f32[1536,128]{1,0:T(8,128)} custom-call(f32[256,8192]{1,0:T(8,128)} %modes_hbm.1, f32[3,64,8192]{2,1,0:T(8,128)} %snaps_hbm.1, f32[128,8192]{1,0:T(8,128)} %probes_ref.1), custom_call_target="tpu_custom_call" | custom-call | tf_op jit(solution)/shard_map/grams/pallas_call | solution.py:244
  18.8 0.0 copy-start
  18.8 1.1 constant_dynamic-slice_fusion.3
  19.8 0.5 collective-permute-start
  20.3 1.3 %collective-permute-done = f32[768,128]{1,0:T(8,128)S(1)} collective-permute-done((f32[768,128]{1,0:T(8,128)S(1)}, f32[768,128]{1,0:T(8,128)S(1)}, u32[]{:S(2)}, u32[]{:S(2)}) %collective-permute-start) | collective-permute-done | bytes 393248 | tf_op jit(solution)/shard_map/ppermute | solution.py:268
  21.7 1.0 dynamic-slice_add_fusion
  22.8 2.9 %collective-permute-start.1 = (f32[192,128]{1,0:T(8,128)S(1)}, f32[192,128]{1,0:T(8,128)S(1)}, u32[]{:S(2)}, u32[]{:S(2)}) collective-permute-start(f32[192,128]{1,0:T(8,128)S(1)} %get-tuple-element.15), channel_id=1, source_target_pairs={{0,2},{1,3},{2,0},{3,1},{4,6},{5,7},{6,4},{7,5},{8,10},{9,11},{10,... | collective-permute-start | bytes 294920 | tf_op jit(solution)/shard_map/ppermute | solution.py:268
  25.7 1.5 %collective-permute-start.3 = (f32[192,128]{1,0:T(8,128)S(1)}, f32[192,128]{1,0:T(8,128)S(1)}, u32[]{:S(2)}, u32[]{:S(2)}) collective-permute-start(f32[192,128]{1,0:T(8,128)S(1)} %get-tuple-element.16), channel_id=1, source_target_pairs={{0,6},{1,7},{2,4},{3,5},{4,2},{5,3},{6,0},{7,1},{8,14},{9,15},{10,... | collective-permute-start | bytes 294920 | tf_op jit(solution)/shard_map/ppermute | solution.py:268
  27.2 0.0 collective-permute-start.2
  27.2 1.6 %collective-permute-done.1 = f32[192,128]{1,0:T(8,128)S(1)} collective-permute-done((f32[192,128]{1,0:T(8,128)S(1)}, f32[192,128]{1,0:T(8,128)S(1)}, u32[]{:S(2)}, u32[]{:S(2)}) %collective-permute-start.1) | collective-permute-done | bytes 98336 | tf_op jit(solution)/shard_map/ppermute | solution.py:268
  28.9 3.4 %collective-permute-done.3 = f32[192,128]{1,0:T(8,128)S(1)} collective-permute-done((f32[192,128]{1,0:T(8,128)S(1)}, f32[192,128]{1,0:T(8,128)S(1)}, u32[]{:S(2)}, u32[]{:S(2)}) %collective-permute-start.3) | collective-permute-done | bytes 98336 | tf_op jit(solution)/shard_map/ppermute | solution.py:268
  32.2 1.3 %collective-permute-done.2 = f32[192,128]{1,0:T(8,128)S(1)} collective-permute-done((f32[192,128]{1,0:T(8,128)S(1)}, f32[192,128]{1,0:T(8,128)S(1)}, u32[]{:S(2)}, u32[]{:S(2)}) %collective-permute-start.2) | collective-permute-done | bytes 98336 | tf_op jit(solution)/shard_map/ppermute | solution.py:268
  33.5 1.6 %collective-permute-start.4 = (f32[192,128]{1,0:T(8,128)S(1)}, f32[192,128]{1,0:T(8,128)S(1)}, u32[]{:S(2)}, u32[]{:S(2)}) collective-permute-start(f32[192,128]{1,0:T(8,128)S(1)} %add_add_fusion), channel_id=1, source_target_pairs={{0,8},{1,9},{2,10},{3,11},{4,12},{5,13},{6,14},{7,15},{8,0},{9,1},... | collective-permute-start | bytes 294920 | tf_op jit(solution)/shard_map/ppermute | solution.py:268
  35.2 3.0 %collective-permute-done.4 = f32[192,128]{1,0:T(8,128)S(1)} collective-permute-done((f32[192,128]{1,0:T(8,128)S(1)}, f32[192,128]{1,0:T(8,128)S(1)}, u32[]{:S(2)}, u32[]{:S(2)}) %collective-permute-start.4) | collective-permute-done | bytes 98336 | tf_op jit(solution)/shard_map/ppermute | solution.py:268
  38.2 2.7 %collective-permute-start.5 = (f32[192,128]{1,0:T(8,128)S(1)}, f32[192,128]{1,0:T(8,128)S(1)}, u32[]{:S(2)}, u32[]{:S(2)}) collective-permute-start(f32[192,128]{1,0:T(8,128)S(1)} %add.63), channel_id=1, source_target_pairs={{0,16},{1,17},{2,18},{3,19},{4,20},{5,21},{6,22},{7,23},{8,24},{9,... | collective-permute-start | bytes 294920 | tf_op jit(solution)/shard_map/ppermute | solution.py:268
  40.9 2.9 %collective-permute-done.5 = f32[192,128]{1,0:T(8,128)S(1)} collective-permute-done((f32[192,128]{1,0:T(8,128)S(1)}, f32[192,128]{1,0:T(8,128)S(1)}, u32[]{:S(2)}, u32[]{:S(2)}) %collective-permute-start.5) | collective-permute-done | bytes 98336 | tf_op jit(solution)/shard_map/ppermute | solution.py:268
  43.8 1.5 %collective-permute-start.8 = (f32[192,128]{1,0:T(8,128)S(1)}, f32[192,128]{1,0:T(8,128)S(1)}, u32[]{:S(2)}, u32[]{:S(2)}) collective-permute-start(f32[192,128]{1,0:T(8,128)S(1)} %add.64), channel_id=1, source_target_pairs={{0,6},{1,7},{2,4},{3,5},{4,2},{5,3},{6,0},{7,1},{8,14},{9,15},{10,... | collective-permute-start | bytes 294920 | tf_op jit(solution)/shard_map/ppermute | solution.py:268
  45.3 1.5 %collective-permute-start.7 = (f32[192,128]{1,0:T(8,128)S(1)}, f32[192,128]{1,0:T(8,128)S(1)}, u32[]{:S(2)}, u32[]{:S(2)}) collective-permute-start(f32[192,128]{1,0:T(8,128)S(1)} %add.64), channel_id=1, source_target_pairs={{0,4},{1,5},{2,6},{3,7},{4,0},{5,1},{6,2},{7,3},{8,12},{9,13},{10,... | collective-permute-start | bytes 294920 | tf_op jit(solution)/shard_map/ppermute | solution.py:268
  46.8 0.5 collective-permute-start.6
  47.4 2.1 %collective-permute-done.8 = f32[192,128]{1,0:T(8,128)S(1)} collective-permute-done((f32[192,128]{1,0:T(8,128)S(1)}, f32[192,128]{1,0:T(8,128)S(1)}, u32[]{:S(2)}, u32[]{:S(2)}) %collective-permute-start.8) | collective-permute-done | bytes 98336 | tf_op jit(solution)/shard_map/ppermute | solution.py:268
  49.5 1.0 collective-permute-done.7
  50.5 1.0 collective-permute-done.6
  51.6 0.1 collective-permute-start.9
  51.7 1.7 %collective-permute-done.9 = f32[768,128]{1,0:T(8,128)S(1)} collective-permute-done((f32[768,128]{1,0:T(8,128)S(1)}, f32[768,128]{1,0:T(8,128)S(1)}, u32[]{:S(2)}, u32[]{:S(2)}) %collective-permute-start.9) | collective-permute-done | bytes 393248 | tf_op jit(solution)/shard_map/ppermute | solution.py:268
  53.4 0.1 broadcast_select_fusion.1
  53.4 0.1 pad_maximum_fusion.packed_ref
  53.5 0.0 copy-done
  53.5 66.4 %core_updates.1 = (f32[256,8192]{1,0:T(8,128)}, f32[256,256]{1,0:T(8,128)}, f32[3,320,256]{2,1,0:T(8,128)}) custom-call(f32[1536,128]{1,0:T(8,128)S(1)} %pad_maximum_fusion.packed_ref, f32[256,256]{1,0:T(8,128)S(1)} %copy-done, f32[256,8192]{1,0:T(8,128)} %modes_hbm.1, f32[3,64,8192]{2,1,0:T(8,128)} %snaps_hbm.1), custom_call_target="tpu_custom_call" | custom-call | tf_op jit(solution)/shard_map/core_updates/pallas_call | solution.py:473
  (7 shorter events, 0.2 us)
Async XLA Ops:
  18.8 34.7 %copy-start = (f32[256,256]{1,0:T(8,128)S(1)}, f32[256,256]{1,0:T(8,128)}, u32[]{:S(2)}) copy-start(f32[256,256]{1,0:T(8,128)} %core_ref.1) | copy-start | bytes 786436
  19.8 1.9 %collective-permute-start = (f32[768,128]{1,0:T(8,128)S(1)}, f32[768,128]{1,0:T(8,128)S(1)}, u32[]{:S(2)}, u32[]{:S(2)}) collective-permute-start(f32[768,128]{1,0:T(8,128)S(1)} %constant_dynamic-slice_fusion.3), channel_id=1, source_target_pairs={{0,1},{1,0},{2,3},{3,2},{4,5},{5,4},{6,7},{7,6},{8,9},{9,8},{10,11... | collective-permute-start | bytes 1179656 | tf_op jit(solution)/shard_map/ppermute | solution.py:268
  22.8 6.1 %collective-permute-start.1 = (f32[192,128]{1,0:T(8,128)S(1)}, f32[192,128]{1,0:T(8,128)S(1)}, u32[]{:S(2)}, u32[]{:S(2)}) collective-permute-start(f32[192,128]{1,0:T(8,128)S(1)} %get-tuple-element.15), channel_id=1, source_target_pairs={{0,2},{1,3},{2,0},{3,1},{4,6},{5,7},{6,4},{7,5},{8,10},{9,11},{10,... | collective-permute-start | bytes 294920 | tf_op jit(solution)/shard_map/ppermute | solution.py:268
  25.7 6.5 %collective-permute-start.3 = (f32[192,128]{1,0:T(8,128)S(1)}, f32[192,128]{1,0:T(8,128)S(1)}, u32[]{:S(2)}, u32[]{:S(2)}) collective-permute-start(f32[192,128]{1,0:T(8,128)S(1)} %get-tuple-element.16), channel_id=1, source_target_pairs={{0,6},{1,7},{2,4},{3,5},{4,2},{5,3},{6,0},{7,1},{8,14},{9,15},{10,... | collective-permute-start | bytes 294920 | tf_op jit(solution)/shard_map/ppermute | solution.py:268
  27.2 6.3 %collective-permute-start.2 = (f32[192,128]{1,0:T(8,128)S(1)}, f32[192,128]{1,0:T(8,128)S(1)}, u32[]{:S(2)}, u32[]{:S(2)}) collective-permute-start(f32[192,128]{1,0:T(8,128)S(1)} %get-tuple-element.17), channel_id=1, source_target_pairs={{0,4},{1,5},{2,6},{3,7},{4,0},{5,1},{6,2},{7,3},{8,12},{9,13},{10,... | collective-permute-start | bytes 294920 | tf_op jit(solution)/shard_map/ppermute | solution.py:268
  33.5 4.7 %collective-permute-start.4 = (f32[192,128]{1,0:T(8,128)S(1)}, f32[192,128]{1,0:T(8,128)S(1)}, u32[]{:S(2)}, u32[]{:S(2)}) collective-permute-start(f32[192,128]{1,0:T(8,128)S(1)} %add_add_fusion), channel_id=1, source_target_pairs={{0,8},{1,9},{2,10},{3,11},{4,12},{5,13},{6,14},{7,15},{8,0},{9,1},... | collective-permute-start | bytes 294920 | tf_op jit(solution)/shard_map/ppermute | solution.py:268
  38.2 5.6 %collective-permute-start.5 = (f32[192,128]{1,0:T(8,128)S(1)}, f32[192,128]{1,0:T(8,128)S(1)}, u32[]{:S(2)}, u32[]{:S(2)}) collective-permute-start(f32[192,128]{1,0:T(8,128)S(1)} %add.63), channel_id=1, source_target_pairs={{0,16},{1,17},{2,18},{3,19},{4,20},{5,21},{6,22},{7,23},{8,24},{9,... | collective-permute-start | bytes 294920 | tf_op jit(solution)/shard_map/ppermute | solution.py:268
  43.8 5.6 %collective-permute-start.8 = (f32[192,128]{1,0:T(8,128)S(1)}, f32[192,128]{1,0:T(8,128)S(1)}, u32[]{:S(2)}, u32[]{:S(2)}) collective-permute-start(f32[192,128]{1,0:T(8,128)S(1)} %add.64), channel_id=1, source_target_pairs={{0,6},{1,7},{2,4},{3,5},{4,2},{5,3},{6,0},{7,1},{8,14},{9,15},{10,... | collective-permute-start | bytes 294920 | tf_op jit(solution)/shard_map/ppermute | solution.py:268
  45.3 5.1 %collective-permute-start.7 = (f32[192,128]{1,0:T(8,128)S(1)}, f32[192,128]{1,0:T(8,128)S(1)}, u32[]{:S(2)}, u32[]{:S(2)}) collective-permute-start(f32[192,128]{1,0:T(8,128)S(1)} %add.64), channel_id=1, source_target_pairs={{0,4},{1,5},{2,6},{3,7},{4,0},{5,1},{6,2},{7,3},{8,12},{9,13},{10,... | collective-permute-start | bytes 294920 | tf_op jit(solution)/shard_map/ppermute | solution.py:268
  46.8 4.6 %collective-permute-start.6 = (f32[192,128]{1,0:T(8,128)S(1)}, f32[192,128]{1,0:T(8,128)S(1)}, u32[]{:S(2)}, u32[]{:S(2)}) collective-permute-start(f32[192,128]{1,0:T(8,128)S(1)} %add.64), channel_id=1, source_target_pairs={{0,2},{1,3},{2,0},{3,1},{4,6},{5,7},{6,4},{7,5},{8,10},{9,11},{10,... | collective-permute-start | bytes 294920 | tf_op jit(solution)/shard_map/ppermute | solution.py:268
  51.6 1.8 %collective-permute-start.9 = (f32[768,128]{1,0:T(8,128)S(1)}, f32[768,128]{1,0:T(8,128)S(1)}, u32[]{:S(2)}, u32[]{:S(2)}) collective-permute-start(f32[768,128]{1,0:T(8,128)S(1)} %pad_maximum_fusion.2), channel_id=1, source_target_pairs={{0,1},{1,0},{2,3},{3,2},{4,5},{5,4},{6,7},{7,6},{8,9},{9,8},{10,11... | collective-permute-start | bytes 1179656 | tf_op jit(solution)/shard_map/ppermute | solution.py:268
